TPU v7x, 32 devices: a whole 2x2x4 slice. The times are simulated.
32 devices in a mesh: rows: 4 (over z), cols: 8 (over y, x, core).
Axes of the slice: x: 2, y: 2, z: 4, core: 2. Of those that a mesh axis runs over, the one named last changes fastest.
Arguments:
- embeddings: bfloat16 [229376, 1024], P(('rows', 'cols'))
- factor_cols: bfloat16 [229376, 512], P(('rows', 'cols')), may hold values from -0.12 to 0.12, as said below
- solved: int32 [229376], P(('rows', 'cols')), may hold values from 0 to 16
- pivots: int32 [256], replicated, may hold values from 0 to 229375, as said below
Outputs:
- new_cols: bfloat16 [229376, 256], P(('rows', 'cols'))
- gains: float32 [229376], P(('rows', 'cols'))
- best_gain: float32 [], replicated
Inputs may be any that keep to these rules, and one draw needn't show every extreme that they name: `pivots`: 256 distinct row numbers in increasing order; the 7168 consecutive rows of one device hold at most 16 of them, and some device holds exactly 16. `factor_cols`: the pivots' factor rows F satisfy: every eigenvalue of F F^T is below 1.
All inputs are finite; a program needn't handle non-finite values.
Results may differ from a plain program's by a relative error of at most 0.001.
Values may be sent and summed in bfloat16 or wider, within the bound.
A program may use at most 128 MiB of HBM per device.

v0:
```python
import jax
import jax.numpy as jnp
from jax import lax
from jax.sharding import PartitionSpec as P

PMAX = 16


EPS = 1e-06
TAU = 6.0
RIDGE = 1.0


def learn(counts):
    c = counts.astype(jnp.float32)
    return (c * (16.0 - c) + 8.0) / 72.0


def scales(emb):
    x = emb.astype(jnp.float32)
    return jnp.sqrt(jnp.mean(x * x, axis=1) + EPS)


def kernel_panel(
    left_emb, left_fac, left_q, left_norm, left_ids, piv_emb, piv_fac, piv_q, piv_norm, pivots
):
    dims = (((1,), (1,)), ((), ()))
    dots = lax.dot_general(left_emb, piv_emb, dims, preferred_element_type=jnp.float32)
    width = left_emb.shape[1] * 1.0
    cosine = dots / (width * left_norm[:, None] * piv_norm[None, :])
    similar = jnp.exp(TAU * (cosine - 1.0))
    ridge = jnp.where(left_ids[:, None] == pivots[None, :], RIDGE, 0.0)
    shared = lax.dot_general(left_fac, piv_fac, dims, preferred_element_type=jnp.float32)
    return left_q[:, None] * piv_q[None, :] * similar + ridge - shared


def body(embeddings, factor_cols, solved, pivots):
    rows_here = embeddings.shape[0]
    total = pivots.shape[0]
    device = lax.axis_index(("rows", "cols"))
    first_row = device * rows_here
    owner = pivots // rows_here
    before = jnp.sum((owner < device).astype(jnp.int32))
    mine = jnp.sum((owner == device).astype(jnp.int32))
    ranks = jnp.arange(PMAX, dtype=jnp.int32)
    valid = ranks < mine
    position = jnp.clip(before + ranks, 0, total - 1)
    local_idx = jnp.clip(pivots[position] - first_row, 0, rows_here - 1)
    keep = valid[:, None]
    own_emb = jnp.where(keep, embeddings[local_idx], 0)
    own_fac = jnp.where(keep, factor_cols[local_idx], 0)
    own_count = jnp.where(valid, solved[local_idx], 0).astype(jnp.bfloat16)
    all_emb, all_fac, all_count = (
        lax.all_gather(own_emb, ("rows", "cols"), axis=0, tiled=True),
        lax.all_gather(own_fac, ("rows", "cols"), axis=0, tiled=True),
        lax.all_gather(own_count, ("rows", "cols"), axis=0, tiled=True),
    )
    earlier = jnp.sum((owner[None, :] < owner[:, None]).astype(jnp.int32), axis=1)
    slot_index = owner * PMAX + jnp.arange(total, dtype=jnp.int32) - earlier
    piv_emb = all_emb[slot_index]
    piv_fac = all_fac[slot_index]
    piv_count = all_count[slot_index].astype(jnp.float32)
    row_q = learn(solved)
    piv_q = learn(piv_count)
    piv_norm = scales(piv_emb)
    row_ids = first_row + jnp.arange(rows_here, dtype=jnp.int32)
    panel = kernel_panel(
        embeddings,
        factor_cols,
        row_q,
        scales(embeddings),
        row_ids,
        piv_emb,
        piv_fac,
        piv_q,
        piv_norm,
        pivots,
    )
    block = kernel_panel(
        piv_emb, piv_fac, piv_q, piv_norm, pivots, piv_emb, piv_fac, piv_q, piv_norm, pivots
    )
    lower = jnp.linalg.cholesky(block)
    full = jax.scipy.linalg.solve_triangular(lower, panel.T, lower=True).T
    facf = factor_cols.astype(jnp.float32)
    gains = row_q * row_q + RIDGE - jnp.sum(facf * facf, axis=1) - jnp.sum(full * full, axis=1)
    best = lax.pmax(jnp.max(gains), ("rows", "cols"))
    return (full.astype(jnp.bfloat16), gains, best)


def solution(mesh):
    in_specs = (P(("rows", "cols"), None), P(("rows", "cols"), None), P(("rows", "cols")), P())
    out_specs = (P(("rows", "cols"), None), P(("rows", "cols")), P())
    return jax.shard_map(body, mesh=mesh, in_specs=in_specs, out_specs=out_specs, check_vma=False)
```

profile of v0, /device:TPU:0, one launch (start us, length us, event | category | flops | bytes accessed | tf_op | source)
XLA Modules:
  0.0 276.6 jit_solution(496081689720558314)
XLA Ops:
  7.2 0.0 all-gather.2.cloned.1.call-start
  7.2 1.3 fusion.27
  8.6 0.7 fusion.29
  9.2 1.3 gather_fusion
  10.6 0.7 iota_compare_fusion.3
  11.2 7.7 %gather_fusion.3 = bf16[16,1024]{1,0:T(8,128)(2,1)S(1)} fusion(bf16[7168,1024]{1,0:T(8,128)(2,1)} %param.4, s32[1024]{0:T(1024)S(1)} %pad_clamp_fusion.1), kind=kCustom, calls=%fused_computation.3 | custom fusion | bytes 65600 | tf_op jit(solution)/shard_map/gather | solution.py:50
  18.9 0.7 broadcast_select_fusion
  19.6 0.0 all-gather.2.cloned.1.call-update
  19.7 0.2 convert_reduce_fusion
  19.9 4.6 %gather_fusion.5 = bf16[16,512]{1,0:T(8,128)(2,1)S(1)} fusion(bf16[7168,512]{1,0:T(8,128)(2,1)} %param.5, s32[1024]{0:T(1024)S(1)} %pad_clamp_fusion.1), kind=kCustom, calls=%fused_computation.5 | custom fusion | bytes 32832 | tf_op jit(solution)/shard_map/gather | solution.py:51
  24.5 0.1 broadcast_select_fusion.1
  24.6 44.7 %all_gather.11 = bf16[512,512]{1,0:T(8,128)(2,1)S(1)} all-gather(bf16[16,512]{1,0:T(8,128)(2,1)S(1)} %broadcast_select_fusion.1), channel_id=1, replica_groups=mesh['rows'=4,'cols'=8] {'rows','cols'}, dimensions={0}, use_global_device_ids=true | all-gather | bytes 540672 | tf_op jit(solution)/shard_map/all_gather | solution.py:55
  69.2 1.2 gather_fusion.6
  70.4 0.3 fusion.34
  70.6 1.4 gather_fusion.1
  72.1 0.7 select_convert_fusion
  72.7 0.1 copy.14
  72.9 0.2 dynamic-update-slice.11
  73.1 36.9 %all-reduce.1 = bf16[512]{0:T(512)(128)(2,1)S(1)} all-reduce(bf16[512]{0:T(512)(128)(2,1)S(1)} %dynamic-update-slice.11), channel_id=1, replica_groups=mesh['rows'=4,'cols'=8] {'rows','cols'}, use_global_device_ids=true, to_apply=%add.1 | all-reduce | flops 512 | bytes 2048
  110.0 2.1 gather_fusion.2
  112.2 0.0 copy-start.1
  112.2 8.1 %multiply_reduce_fusion = f32[7168]{0:T(1024)S(1)} fusion(bf16[7168,1024]{1,0:T(8,128)(2,1)} %param.4), kind=kLoop, calls=%fused_computation.9 | loop fusion | flops 22012928 | bytes 14708736 | tf_op jit(solution)/shard_map/reduce_sum | solution.py:21
  120.3 0.0 copy-done.1
  120.3 0.0 copy-start
  120.3 4.6 %multiply_reduce_fusion.1 = f32[7168]{0:T(1024)S(1)} fusion(bf16[7168,512]{1,0:T(8,128)(2,1)} %param.5), kind=kLoop, calls=%fused_computation.10 | loop fusion | flops 11002880 | bytes 7368704 | tf_op jit(solution)/shard_map/reduce_sum | solution.py:85
  125.0 0.0 all-gather.2.cloned.1.call-done
  125.0 2.9 %gather_fusion.4 = bf16[256,1024]{1,0:T(8,128)(2,1)S(1)} fusion(bf16[512,1024]{1,0:T(8,128)(2,1)} %all-gather.2.cloned.1.call-done, s32[1024]{0:T(1024)S(1)} %pad_clamp_fusion), kind=kCustom, calls=%fused_computation.4 | custom fusion | bytes 1049600 | tf_op jit(solution)/shard_map/gather | solution.py:60
  127.9 0.2 multiply_reduce_fusion.3
  128.1 0.3 fusion.33
  128.4 0.1 copy.13
  128.6 0.0 copy-done
  128.6 0.3 fusion.12
  128.9 11.7 %cholesky.49 = f32[128,128]{1,0:T(8,128)S(1)} custom-call(f32[128,128]{1,0:T(8,128)S(1)} %cholesky.115), custom_call_target="Cholesky" | custom-call | tf_op jit(solution)/shard_map/jit(cholesky)/cholesky | solution.py:82
  140.7 10.0 %custom-call.15 = f32[1,128,128]{1,2,0:T(8,128)S(1)} custom-call(f32[1,128,128]{2,1,0:T(8,128)S(1)} %get-tuple-element.38), custom_call_target="InvertDiagBlocksLowerTriangular" | custom-call | tf_op jit(solution)/shard_map/jit(cholesky)/cholesky | solution.py:82
  150.7 0.2 constant_dynamic-update-slice_fusion.1
  150.9 0.3 convolution_subtract_fusion.2
  151.2 11.7 %cholesky.103 = f32[128,128]{1,0:T(8,128)S(1)} custom-call(f32[128,128]{1,0:T(8,128)S(1)} %convolution_subtract_fusion.2), custom_call_target="Cholesky" | custom-call | tf_op jit(solution)/shard_map/jit(cholesky)/cholesky | solution.py:82
  162.9 0.6 compare_reduce_fusion
  164.9 0.1 triangular_solve.60
  165.0 4.0 %while.1 = (s32[]{:T(128)}, f32[256,256]{1,0:T(8,128)S(1)}, s32[2,2]{1,0:T(2,128)S(1)}, f32[2,128,128]{2,1,0:T(8,128)S(1)}, s32[]{:T(128)}) while((s32[]{:T(128)}, f32[256,256]{1,0:T(8,128)S(1)}, s32[2,2]{1,0:T(2,128)S(1)}, f32[2,128,128]{2,1,0:T(8,128)S(1)}, s32[]{:T(128)}) %tuple.35), condition=%wide.while_cond, body=%wide.while_body.sunk | while | flops 2 | bytes 131181 | solution.py:83
  165.0 0.6 fusion.48
  165.6 1.4 bitcast_dynamic-update-slice_fusion.2
  167.0 0.6 fusion.48
  167.6 1.4 bitcast_dynamic-update-slice_fusion.2
  169.0 19.7 %custom-call.16 = f32[2,128,128]{1,2,0:T(8,128)S(1)} custom-call(f32[2,128,128]{2,1,0:T(8,128)S(1)} %get-tuple-element.10), custom_call_target="InvertDiagBlocksLowerTriangular" | custom-call | tf_op jit(solution)/shard_map/jit(_solve_triangular)/triangular_solve | solution.py:83
  188.7 11.4 %fusion.4 = f32[256,7168]{1,0:T(8,128)} fusion(bf16[256,1024]{1,0:T(8,128)(2,1)S(1)} %gather_fusion.4, bf16[7168,1024]{1,0:T(8,128)(2,1)} %param.4, s32[7168]{0:T(1024)S(1)} %iota_add_fusion, f32[256]{0:T(256)S(1)} %get-tuple-element.40, f32[7168]{0:T(1024)S(1)} %get-tuple-element.44, f32[256]{0:T(256)S(1)} %fusion.26, f32[7168]{0:T(1024)S(1)} %get-tuple-element.43, ...), kind=kOutput, calls=%fused_computation.18 | convolution fusion | flops 3774611456 | bytes 22633472 | tf_op jit(solution)/shard_map/dot_general | solution.py:28
  200.0 7.3 %convolution_subtract_fusion = f32[256,7168]{1,0:T(8,128)S(1)} fusion(f32[256,7168]{1,0:T(8,128)} %fusion.4, bf16[256,512]{1,0:T(8,128)(2,1)S(1)} %gather_fusion.6, bf16[7168,512]{1,0:T(8,128)(2,1)} %param.5), kind=kOutput, calls=%fused_computation.11 | convolution fusion | flops 1880883200 | bytes 22282240 | tf_op jit(solution)/shard_map/dot_general | solution.py:33
  207.3 3.5 %fusion.7 = f32[128,7168]{1,0:T(8,128)S(1)} fusion(f32[256,7168]{1,0:T(8,128)S(1)} %convolution_subtract_fusion, f32[2,128,128]{1,2,0:T(8,128)S(1)} %custom-call.16), kind=kOutput, calls=%fused_computation.23 | convolution fusion | flops 1409286144 | bytes 7405568 | tf_op jit(solution)/shard_map/jit(_solve_triangular)/triangular_solve | solution.py:83
  210.8 3.6 %convolution_subtract_fusion.1 = f32[128,7168]{1,0:T(8,128)S(1)} fusion(f32[128,7168]{1,0:T(8,128)S(1)} %fusion.7, f32[256,7168]{1,0:T(8,128)S(1)} %convolution_subtract_fusion, f32[256,256]{1,0:T(8,128)S(1)} %get-tuple-element.93), kind=kOutput, calls=%fused_computation.12 | convolution fusion | flops 1410203648 | bytes 11075584 | tf_op jit(solution)/shard_map/jit(_solve_triangular)/triangular_solve | solution.py:83
  214.5 3.5 %fusion.19 = f32[128,7168]{1,0:T(8,128)S(1)} fusion(f32[128,7168]{1,0:T(8,128)S(1)} %convolution_subtract_fusion.1, f32[2,128,128]{1,2,0:T(8,128)S(1)} %custom-call.16), kind=kOutput, calls=%fused_computation.44 | convolution fusion | flops 1409286144 | bytes 7405568 | tf_op jit(solution)/shard_map/jit(_solve_triangular)/triangular_solve | solution.py:83
  218.0 0.6 multiply_reduce_fusion.2
  218.6 2.3 fusion.6
  220.9 1.2 fusion.31
  222.1 41.4 %pmax.7 = f32[]{:T(128)} all-reduce(f32[]{:T(128)} %get-tuple-element.30), channel_id=1, replica_groups=mesh['rows'=4,'cols'=8] {'rows','cols'}, use_global_device_ids=true, to_apply=%region_12.13 | all-reduce | flops 1 | bytes 8 | tf_op jit(solution)/shard_map/pmax | solution.py:86
  263.5 5.9 %copy.15 = bf16[7168,256]{1,0:T(8,128)(2,1)} copy(bf16[7168,256]{0,1:T(8,128)(2,1)} %fusion.6) | data formatting | bytes 7340032
  (19 shorter events, 0.2 us)
Async XLA Ops:
  7.2 117.8 %all-gather.2.cloned.1.call-start = ((), (), s32[]{:S(2)}) async-start(), calls=%async_computation | async-start | bytes 1081344 | tf_op jit(solution)/shard_map/all_gather | solution.py:54
  112.2 8.1 %copy-start.1 = (s32[7168]{0:T(1024)S(1)}, s32[7168]{0:T(1024)}, u32[]{:S(2)}) copy-start(s32[7168]{0:T(1024)} %param.6) | copy-start | bytes 86020
  120.3 8.3 %copy-start = (s32[256]{0:T(256)S(1)}, s32[256]{0:T(256)}, u32[]{:S(2)}) copy-start(s32[256]{0:T(256)} %param.7) | copy-start | bytes 3076
Sparse Core Ops, SparseCore 0:
  19.8 56.6 all-gather.1
where the time goes:
time: 282 us; the launch traced here: 277 us
  blocking collectives  123 us (44%)
  other arithmetic  75.5 us (27%)
  local copies, waits for them, and re-layouts  31.7 us (11%)
  matrix products  30.3 us (11%)
  between operations  16.1 us (6%)
    all_gather x1, blocking collectives, body(): lax.all_gather(own_fac, ('rows', 'cols'), axis=0, tiled=True)  44.7 us
    pmax x1, blocking collectives, body(): best = lax.pmax(jnp.max(gains), ('rows', 'cols'))  41.4 us
    unnamed x1, blocking collectives  36.9 us
    another operation x6, other arithmetic, body(): lower = jnp.linalg.cholesky(block)  34.1 us
    another operation x3, other arithmetic, body(): full = jax.scipy.linalg.solve_triangular(lower, panel.T, lower=True).T  19.7 us
    dot_general x2, matrix products, kernel_panel(): lax.dot_general(left_emb, piv_emb, dims, preferred_element_type=jnp.float32)  11.7 us
    another operation x3, matrix products, body(): full = jax.scipy.linalg.solve_triangular(lower, panel.T, lower=True).T  10.6 us
    reduce_sum x2, other arithmetic, scales(): return jnp.sqrt(jnp.mean(x * x, axis=1) + EPS)  8.29 us
  transfers between devices with their start and end apart: 1, of which 0 were waited for; matrix products, arithmetic and copies ran while one was open for 9% of the time, Pallas kernels for 0%

commit v1 on v0

v1 whole, which is shorter than its diff:
```python
import functools

import jax
import jax.numpy as jnp
from jax import lax
from jax.experimental import pallas as pl
from jax.experimental.pallas import tpu as pltpu
from jax.sharding import PartitionSpec as P

PMAX = 16
EPS = 1e-06
TAU = 6.0
RIDGE = 1.0
LANES = 128
GROUP = 8
TILE = 1024
SUB = 256
VMEM_LIMIT = 56 * 1024 * 1024
MESH = pl.DeviceIdType.MESH
NT = (((1,), (1,)), ((), ()))


def learn(counts):
    c = counts.astype(jnp.float32)
    return (c * (16.0 - c) + 8.0) / 72.0


def pick_kernel(n_cols, piv_ref, solved_ref, emb_ref, fac_ref, out_ref, ebuf, fbuf, sem):
    rows_here, width = emb_ref.shape
    fac_width = fac_ref.shape[1]
    total = piv_ref.shape[0]
    first = (lax.axis_index("rows") * n_cols + lax.axis_index("cols")) * rows_here
    before = jnp.int32(0)
    step = 1
    while step * 2 <= total:
        step *= 2
    while step:
        probe = jnp.minimum(before + step - 1, total - 1)
        inside = before + step <= total
        before = before + jnp.where(inside & (piv_ref[probe] < first), step, 0)
        step //= 2
    copies = []
    spots = []
    for r in range(PMAX):
        idx = jnp.clip(piv_ref[jnp.minimum(before + r, total - 1)] - first, 0, rows_here - 1)
        base = pl.multiple_of(lax.shift_left(lax.shift_right_logical(idx, 4), 4), 16)
        for src, dst, k in ((emb_ref, ebuf, 0), (fac_ref, fbuf, 1)):
            copy = pltpu.make_async_copy(
                src.at[pl.ds(base, 16), :], dst.at[pl.ds(16 * r, 16), :], sem.at[k, r]
            )
            copy.start()
            copies.append(copy)
        spots.append((idx, idx - base + 16 * r))
    row = lax.broadcasted_iota(jnp.int32, (PMAX, 16 * PMAX), 0)
    lane = lax.broadcasted_iota(jnp.int32, (PMAX, 16 * PMAX), 1)
    row1 = lax.broadcasted_iota(jnp.int32, (PMAX, LANES), 0)
    want = jnp.zeros((PMAX, 16 * PMAX), jnp.int32)
    count = jnp.zeros((PMAX, LANES), jnp.int32)
    for r, (idx, spot) in enumerate(spots):
        want = jnp.where(row == r, spot, want)
        count = jnp.where(row1 == r, solved_ref[idx], count)
    pick = jnp.where(lane == want, 1.0, 0.0).astype(jnp.bfloat16)
    out_ref[:, width + fac_width:] = count.astype(jnp.float32).astype(jnp.bfloat16)
    for copy in copies:
        copy.wait()
    out_ref[:, :width] = jnp.dot(
        pick, ebuf[...], preferred_element_type=jnp.float32
    ).astype(jnp.bfloat16)
    out_ref[:, width:width + fac_width] = jnp.dot(
        pick, fbuf[...], preferred_element_type=jnp.float32
    ).astype(jnp.bfloat16)


def gather_kernel(n_rows, n_cols, own_ref, out_ref, send_sem, recv_sem, own_sem):
    r = lax.axis_index("rows")
    c = lax.axis_index("cols")
    pairs = n_cols // 2
    h = c // 2
    k = c - 2 * h
    twin = 2 * h + 1 - k

    def other_row(j):
        return lax.rem(r + j, n_rows)

    def other_col(i):
        return 2 * lax.rem(h + i, pairs) + k

    barrier = pltpu.get_barrier_semaphore()
    peers = [(other_row(j), c) for j in range(1, n_rows)]
    peers += [(r, other_col(i)) for i in range(1, pairs)]
    peers.append((r, twin))
    for peer in peers:
        pl.semaphore_signal(barrier, inc=1, device_id=peer, device_id_type=MESH)
    own = pltpu.make_async_copy(own_ref, out_ref.at[r * n_cols + c], own_sem)
    own.start()
    pl.semaphore_wait(barrier, len(peers))

    sent = []

    def send(src, block, peer):
        copy = pltpu.make_async_remote_copy(
            src_ref=src,
            dst_ref=out_ref.at[block],
            send_sem=send_sem.at[len(sent)],
            recv_sem=recv_sem.at[block],
            device_id=peer,
            device_id_type=MESH,
        )
        copy.start()
        sent.append(copy)

    def arrived(block):
        pltpu.make_async_remote_copy(
            src_ref=own_ref,
            dst_ref=out_ref.at[block],
            send_sem=send_sem.at[0],
            recv_sem=recv_sem.at[block],
            device_id=(r, twin),
            device_id_type=MESH,
        ).wait_recv()

    me = r * n_cols + c
    for i in range(1, pairs):
        send(own_ref, me, (r, other_col(i)))
    for j in range(1, n_rows):
        send(own_ref, me, (other_row(j), c))
    send(own_ref, me, (r, twin))
    order = [j for j in range(1, n_rows)]
    for j in order:
        block = other_row(j) * n_cols + c
        arrived(block)
        for i in range(1, pairs):
            send(out_ref.at[block], block, (r, other_col(i)))
        send(out_ref.at[block], block, (r, twin))
    for j in [0] + order:
        for i in range(1, pairs):
            block = other_row(j) * n_cols + other_col(i)
            arrived(block)
            send(out_ref.at[block], block, (r, twin))
    for j in range(n_rows):
        for i in range(pairs):
            arrived(other_row(j) * n_cols + 2 * lax.rem(h + i, pairs) + 1 - k)
    own.wait()
    for copy in sent:
        copy.wait_send()


def split(x):
    hi = x.astype(jnp.bfloat16)
    return hi, (x - hi.astype(jnp.float32)).astype(jnp.bfloat16)


def factor_kernel(
    rows_here, width, fac_width, piv_ref, all_ref, out_ref, hi_ref, lo_ref, side_ref, work
):
    total = piv_ref.shape[1]
    slots = all_ref.shape[0]
    f32 = jnp.float32
    sub = lax.broadcasted_iota(jnp.int32, (total, total), 0)
    lane = lax.broadcasted_iota(jnp.int32, (total, total), 1)
    eye = sub == lane
    ids = jnp.broadcast_to(piv_ref[...].astype(f32), (total, total))
    ids = jnp.sum(jnp.where(eye, ids, 0.0), axis=1, keepdims=True)
    place = lax.broadcasted_iota(jnp.int32, (total, slots), 0)
    slot = lax.broadcasted_iota(jnp.int32, (total, slots), 1)
    owner = lax.shift_right_logical(slot, PMAX.bit_length() - 1)
    low = (owner * rows_here).astype(f32)
    above = ids >= low
    before = total - jnp.sum(jnp.where(above, 1.0, 0.0), axis=0, keepdims=True)
    rank = place.astype(f32) - before
    chosen = above & (ids < low + rows_here) & (rank == (slot - owner * PMAX).astype(f32))
    chosen = jnp.where(chosen, 1.0, 0.0).astype(jnp.bfloat16)
    full_width = all_ref.shape[1]
    part = width // 2
    for start in range(0, full_width, part):
        size = min(part, full_width - start)
        out_ref[:, start:start + size] = jnp.dot(
            chosen, all_ref[:, start:start + size], preferred_element_type=f32
        ).astype(jnp.bfloat16)
    emb = out_ref[:, :width]
    fac = out_ref[:, width:width + fac_width]
    count = out_ref[:, width + fac_width:width + fac_width + 1].astype(f32)
    wide = emb.astype(f32)
    norm = lax.rsqrt(jnp.sum(wide * wide, axis=1, keepdims=True) / width + EPS)
    q = learn(count)

    def to_row(col):
        return jnp.sum(jnp.where(eye, col, 0.0), axis=0, keepdims=True)

    norm_row = to_row(norm) * (TAU / width)
    q_row = to_row(q)
    side_ref[0:1, :] = norm_row
    side_ref[1:2, :] = q_row
    dots = lax.dot_general(emb, emb, NT, preferred_element_type=f32)
    shared = lax.dot_general(fac, fac, NT, preferred_element_type=f32)
    block = q * q_row * jnp.exp(dots * norm * norm_row - TAU) - shared
    work[...] = block + jnp.where(eye, RIDGE, 0.0)

    row8 = lax.broadcasted_iota(jnp.int32, (GROUP, total), 0)
    lane8 = lax.broadcasted_iota(jnp.int32, (GROUP, total), 1)

    def step(b, carry):
        start = pl.multiple_of(b * GROUP, GROUP)
        rows = work[pl.ds(start, GROUP), :]
        cols = [
            jnp.broadcast_to(
                jnp.sum(jnp.where(lane8 == start + i, rows, 0.0), axis=1, keepdims=True),
                (GROUP, total),
            )
            for i in range(GROUP)
        ]
        left = jnp.where(lane8 >= start + GROUP, rows, 0.0)
        solved = jnp.where(
            (lane8 >= start) & (lane8 < start + GROUP),
            jnp.where(lane8 == start + row8, 1.0, 0.0),
            rows,
        )
        diag = jnp.ones((GROUP, total), f32)
        for i in range(GROUP):
            d = cols[i][i:i + 1, :]
            diag = jnp.where(row8 == i, d, diag)
            m = jnp.where(row8 > i, cols[i] * (1.0 / d), 0.0)
            for n in range(i + 1, GROUP):
                cols[n] = cols[n] - m * cols[n][i:i + 1, :]
            solved = solved - m * solved[i:i + 1, :]
            left = left - m * left[i:i + 1, :]
        scale = lax.rsqrt(diag)
        solved = solved * scale
        left = left * scale
        delta = lax.dot_general(
            left, solved, (((0,), (0,)), ((), ())),
            precision=lax.Precision.HIGHEST, preferred_element_type=f32,
        )
        keep = jnp.where((lane >= start) & (lane < start + GROUP), 0.0, work[...])
        work[...] = keep - delta
        work[pl.ds(start, GROUP), :] = solved
        return carry

    lax.fori_loop(0, total // GROUP, step, 0)
    hi, lo = split(work[...])
    hi_ref[...] = hi
    lo_ref[...] = lo


def panel_kernel(
    n_cols, rows_here, width, fac_width,
    emb_ref, fac_ref, solved_ref, piv_ref, ids_ref, hi_ref, lo_ref, side_ref,
    new_ref, gain_ref, best_ref,
):
    f32 = jnp.float32
    total = ids_ref.shape[1]
    tile = emb_ref.shape[0]
    step = pl.program_id(0)
    first = (lax.axis_index("rows") * n_cols + lax.axis_index("cols")) * rows_here + step * tile
    piv_emb = piv_ref[:, :width]
    piv_fac = piv_ref[:, width:width + fac_width]
    hi_w = hi_ref[...]
    lo_w = lo_ref[...]
    norm_row = side_ref[0:1, :]
    q_row = side_ref[1:2, :]
    ids = ids_ref[...] - first
    sub = lax.broadcasted_iota(jnp.int32, (LANES, LANES), 0)
    lane = lax.broadcasted_iota(jnp.int32, (LANES, LANES), 1)
    eye = sub == lane
    row = lax.broadcasted_iota(jnp.int32, (SUB, total), 0)
    q_lanes = learn(solved_ref[...])
    best = jnp.full((1, LANES), -jnp.inf, f32)
    for s in range(0, tile, SUB):
        emb = emb_ref[s:s + SUB, :]
        fac = fac_ref[s:s + SUB, :]
        dots = lax.dot_general(emb, piv_emb, NT, preferred_element_type=f32)
        shared = lax.dot_general(fac, piv_fac, NT, preferred_element_type=f32)
        wide = emb.astype(f32)
        norm = lax.rsqrt(jnp.sum(wide * wide, axis=1, keepdims=True) / width + EPS)
        widef = fac.astype(f32)
        used = jnp.sum(widef * widef, axis=1, keepdims=True)
        q = jnp.concatenate(
            [
                jnp.sum(
                    jnp.where(eye, q_lanes[g:g + 1, :], 0.0), axis=1, keepdims=True
                )
                for g in range(s // LANES, (s + SUB) // LANES)
            ],
            axis=0,
        )
        panel = q * q_row * jnp.exp(dots * norm * norm_row - TAU) - shared
        panel = jnp.where(row + s == ids, panel + RIDGE, panel)
        hi, lo = split(panel)
        full = (
            lax.dot_general(hi, hi_w, NT, preferred_element_type=f32)
            + lax.dot_general(hi, lo_w, NT, preferred_element_type=f32)
            + lax.dot_general(lo, hi_w, NT, preferred_element_type=f32)
        )
        new_ref[s:s + SUB, :] = full.astype(jnp.bfloat16)
        gain = q * q + RIDGE - used - jnp.sum(full * full, axis=1, keepdims=True)
        for g in range(0, SUB, LANES):
            line = jnp.sum(jnp.where(eye, gain[g:g + LANES, :], 0.0), axis=0, keepdims=True)
            at = (s + g) // LANES
            gain_ref[at:at + 1, :] = line
            best = jnp.maximum(best, line)
    best = jnp.broadcast_to(best, best_ref.shape)

    @pl.when(step == 0)
    def _():
        best_ref[...] = best

    @pl.when(step > 0)
    def _():
        best_ref[...] = jnp.maximum(best_ref[...], best)


def best_kernel(n_rows, n_cols, own_ref, out_ref, stage, buf_r, buf_c, send_r, recv_r, send_c, recv_c):
    r = lax.axis_index("rows")
    c = lax.axis_index("cols")
    barrier = pltpu.get_barrier_semaphore()
    peers_r = [(lax.rem(r + j, n_rows), c) for j in range(1, n_rows)]
    peers_c = [(r, lax.rem(c + i, n_cols)) for i in range(1, n_cols)]
    for peer in peers_r + peers_c:
        pl.semaphore_signal(barrier, inc=1, device_id=peer, device_id_type=MESH)
    pl.semaphore_wait(barrier, len(peers_r) + len(peers_c))

    def exchange(src, buf, send_sem, recv_sem, peers):
        copies = []
        for j, peer in enumerate(peers):
            copy = pltpu.make_async_remote_copy(
                src_ref=src, dst_ref=buf.at[j], send_sem=send_sem.at[j],
                recv_sem=recv_sem.at[j], device_id=peer, device_id_type=MESH,
            )
            copy.start()
            copies.append(copy)
        top = src[...]
        for j, copy in enumerate(copies):
            copy.wait_recv()
            top = jnp.maximum(top, buf[j])
        for copy in copies:
            copy.wait_send()
        return top

    stage[...] = exchange(own_ref, buf_r, send_r, recv_r, peers_r)
    out_ref[0, 0] = jnp.max(exchange(stage, buf_c, send_c, recv_c, peers_c))


def body(n_rows, n_cols, embeddings, factor_cols, solved, pivots):
    rows_here, width = embeddings.shape
    fac_width = factor_cols.shape[1]
    total = pivots.shape[0]
    devices = n_rows * n_cols
    packet = width + fac_width + LANES
    bf16 = jnp.bfloat16
    vmem = pl.BlockSpec(memory_space=pltpu.VMEM)
    smem = pl.BlockSpec(memory_space=pltpu.SMEM)
    params = functools.partial(pltpu.CompilerParams, vmem_limit_bytes=VMEM_LIMIT)
    own = pl.pallas_call(
        functools.partial(pick_kernel, n_cols),
        out_shape=jax.ShapeDtypeStruct((PMAX, packet), bf16),
        in_specs=[smem, smem, pl.BlockSpec(memory_space=pl.ANY), pl.BlockSpec(memory_space=pl.ANY)],
        out_specs=vmem,
        scratch_shapes=[
            pltpu.VMEM((16 * PMAX, width), bf16),
            pltpu.VMEM((16 * PMAX, fac_width), bf16),
            pltpu.SemaphoreType.DMA((2, PMAX)),
        ],
        compiler_params=params(),
        name="pick",
    )(pivots, solved, embeddings, factor_cols)
    everyone = pl.pallas_call(
        functools.partial(gather_kernel, n_rows, n_cols),
        out_shape=jax.ShapeDtypeStruct((devices, PMAX, packet), bf16),
        in_specs=[vmem],
        out_specs=vmem,
        scratch_shapes=[
            pltpu.SemaphoreType.DMA((devices,)),
            pltpu.SemaphoreType.DMA((devices,)),
            pltpu.SemaphoreType.DMA,
        ],
        compiler_params=params(collective_id=0, has_side_effects=True),
        name="gather",
    )(own)
    ids = pivots.reshape(1, total)
    piv, hi, lo, side = pl.pallas_call(
        functools.partial(factor_kernel, rows_here, width, fac_width),
        out_shape=[
            jax.ShapeDtypeStruct((total, packet), bf16),
            jax.ShapeDtypeStruct((total, total), bf16),
            jax.ShapeDtypeStruct((total, total), bf16),
            jax.ShapeDtypeStruct((8, total), jnp.float32),
        ],
        in_specs=[vmem, vmem],
        out_specs=[vmem] * 4,
        scratch_shapes=[pltpu.VMEM((total, total), jnp.float32)],
        compiler_params=params(),
        name="factor",
    )(ids, everyone.reshape(devices * PMAX, packet))
    tile = TILE
    lines = rows_here // LANES

    def whole(shape):
        return pl.BlockSpec(shape, lambda t: (0, 0))

    new_cols, gains, best = pl.pallas_call(
        functools.partial(panel_kernel, n_cols, rows_here, width, fac_width),
        out_shape=[
            jax.ShapeDtypeStruct((rows_here, total), bf16),
            jax.ShapeDtypeStruct((lines, LANES), jnp.float32),
            jax.ShapeDtypeStruct((8, LANES), jnp.float32),
        ],
        grid=(rows_here // tile,),
        in_specs=[
            pl.BlockSpec((tile, width), lambda t: (t, 0)),
            pl.BlockSpec((tile, fac_width), lambda t: (t, 0)),
            pl.BlockSpec((tile // LANES, LANES), lambda t: (t, 0)),
            whole((total, packet)),
            whole((1, total)),
            whole((total, total)),
            whole((total, total)),
            whole((8, total)),
        ],
        out_specs=[
            pl.BlockSpec((tile, total), lambda t: (t, 0)),
            pl.BlockSpec((tile // LANES, LANES), lambda t: (t, 0)),
            whole((8, LANES)),
        ],
        compiler_params=params(),
        name="panel",
    )(embeddings, factor_cols, solved.reshape(lines, LANES), piv, ids, hi, lo, side)
    top = pl.pallas_call(
        functools.partial(best_kernel, n_rows, n_cols),
        out_shape=jax.ShapeDtypeStruct((1, 1), jnp.float32),
        in_specs=[vmem],
        out_specs=smem,
        scratch_shapes=[
            pltpu.VMEM((8, LANES), jnp.float32),
            pltpu.VMEM((n_rows, 8, LANES), jnp.float32),
            pltpu.VMEM((n_cols, 8, LANES), jnp.float32),
            pltpu.SemaphoreType.DMA((n_rows,)),
            pltpu.SemaphoreType.DMA((n_rows,)),
            pltpu.SemaphoreType.DMA((n_cols,)),
            pltpu.SemaphoreType.DMA((n_cols,)),
        ],
        compiler_params=params(collective_id=1, has_side_effects=True),
        name="best",
    )(best)
    return new_cols, gains.reshape(rows_here), top.reshape(())


def solution(mesh):
    n_rows, n_cols = mesh.shape["rows"], mesh.shape["cols"]
    in_specs = (P(("rows", "cols"), None), P(("rows", "cols"), None), P(("rows", "cols")), P())
    out_specs = (P(("rows", "cols"), None), P(("rows", "cols")), P())
    return jax.shard_map(
        functools.partial(body, n_rows, n_cols),
        mesh=mesh, in_specs=in_specs, out_specs=out_specs, check_vma=False,
    )
```

time: 282 us -> 82.3 us (0.29); the launches traced: 277 us -> 82.2 us
  blocking collectives: 123 us -> 0 us
  Pallas kernels: 0 us -> 79.7 us
  other arithmetic: 75.5 us -> 0 us
  local copies, waits for them, and re-layouts: 31.7 us -> 0 us
  matrix products: 30.3 us -> 0 us
  between operations: 16.1 us -> 2.41 us
    pallas_call x0 -> x5, Pallas kernels: none -> 79.7 us  [the longest x1 22.3 us: body(): pl.pallas_call(functools.partial(gather_kernel, n_rows, n_cols), out_shap...]
    another operation x9 -> x0, other arithmetic: 53.8 us -> none  [the longest x6 34.1 us: body(): lower = jnp.linalg.cholesky(block)]
    all_gather x1 -> x0, blocking collectives: 44.7 us -> none  [body(): lax.all_gather(own_fac, ('rows', 'cols'), axis=0, tiled=True)]
    pmax x1 -> x0, blocking collectives: 41.4 us -> none  [body(): best = lax.pmax(jnp.max(gains), ('rows', 'cols'))]
    unnamed x1 -> x0, blocking collectives: 36.9 us -> none
    gather x7 -> x0, local copies, waits for them, and re-layouts: 21.2 us -> none  [the longest x1 7.67 us: body(): own_emb = jnp.where(keep, embeddings[local_idx], 0)]
    dot_general x4 -> x0, matrix products: 19.2 us -> none  [the longest x2 11.7 us: kernel_panel(): lax.dot_general(left_emb, piv_emb, dims, preferred_element_type=jnp.float32)]
    reduce_sum x6 -> x0, other arithmetic: 15 us -> none  [the longest x2 8.29 us: scales(): return jnp.sqrt(jnp.mean(x * x, axis=1) + EPS)]
  transfers between devices with their start and end apart: 1 -> 0, of which waited for: 0 -> 0; matrix products, arithmetic and copies ran while one was open for 9% -> 0% of each run, Pallas kernels for 0% -> 0%
where the time goes in v1:
time: 82.3 us; the launch traced here: 82.2 us
  Pallas kernels  79.7 us (97%)
  between operations  2.41 us (3%)
    pallas_call x1, Pallas kernels, body(): pl.pallas_call(functools.partial(gather_kernel, n_rows, n_cols), out_shap...  22.3 us
    pallas_call x1, Pallas kernels, body(): pl.pallas_call(functools.partial(factor_kernel, rows_here, width, fac_wid...  21.9 us
    pallas_call x1, Pallas kernels, body(): pl.pallas_call(functools.partial(panel_kernel, n_cols, rows_here, width,...  21.4 us
    pallas_call x1, Pallas kernels, body(): pl.pallas_call(functools.partial(best_kernel, n_rows, n_cols), out_shape=...  10.3 us
    pallas_call x1, Pallas kernels, body(): pl.pallas_call(functools.partial(pick_kernel, n_cols), out_shape=jax.Shap...  3.71 us

profile of v1, /device:TPU:0, one launch (start us, length us, event | category | flops | bytes accessed | tf_op | source)
XLA Modules:
  0.0 82.2 jit_solution(17935935042642871798)
XLA Ops:
  0.6 3.7 %pick.1.own_ref = bf16[16,1664]{1,0:T(8,128)(2,1)} custom-call(s32[256]{0:T(256)} %piv_ref.1, s32[7168]{0:T(1024)} %solved_ref.1, bf16[7168,1024]{1,0:T(8,128)(2,1)} %emb_ref.3, bf16[7168,512]{1,0:T(8,128)(2,1)} %fac_ref.3), custom_call_target="tpu_custom_call" | custom-call | tf_op jit(solution)/shard_map/pick/pallas_call | solution.py:353
  4.3 22.3 %gather.1 = bf16[32,16,1664]{2,1,0:T(8,128)(2,1)} custom-call(bf16[16,1664]{1,0:T(8,128)(2,1)} %pick.1.own_ref), custom_call_target="tpu_custom_call" | custom-call | tf_op jit(solution)/shard_map/gather/pallas_call | solution.py:366
  26.7 21.9 %factor.1 = (bf16[256,1664]{1,0:T(8,128)(2,1)}, bf16[256,256]{1,0:T(8,128)(2,1)}, bf16[256,256]{1,0:T(8,128)(2,1)}, f32[8,256]{1,0:T(8,128)}) custom-call(s32[1,256]{1,0:T(1,128)} %bitcast.7, bf16[512,1664]{1,0:T(8,128)(2,1)} %bitcast.5), custom_call_target="tpu_custom_call" | custom-call | tf_op jit(solution)/shard_map/factor/pallas_call | solution.py:380
  48.6 21.4 %panel.1 = (bf16[7168,256]{1,0:T(8,128)(2,1)}, f32[56,128]{1,0:T(8,128)}, f32[8,128]{1,0:T(8,128)}) custom-call(bf16[7168,1024]{1,0:T(8,128)(2,1)} %emb_ref.3, bf16[7168,512]{1,0:T(8,128)(2,1)} %fac_ref.3, s32[56,128]{1,0:T(8,128)} %bitcast.6, bf16[256,1664]{1,0:T(8,128)(2,1)} %get-tuple-element.10.piv_ref, s32[1,256]{1,0:T(1,128)} %bitcast.8, ...), custom_call_target="tpu_custom_call" | custom-call | tf_op jit(solution)/shard_map/panel/pallas_call | solution.py:400
  70.1 10.3 %best.1 = f32[1,1]{1,0:T(1,128)} custom-call(f32[8,128]{1,0:T(8,128)} %get-tuple-element.16.own_ref), custom_call_target="tpu_custom_call" | custom-call | tf_op jit(solution)/shard_map/best/pallas_call | solution.py:426

commit v2 on v1

--- a/solution.py
+++ b/solution.py
@@ -11,9 +11,9 @@
 EPS = 1e-06
 TAU = 6.0
 RIDGE = 1.0
+LOG2E = 1.4426950408889634
 LANES = 128
 GROUP = 8
-TILE = 1024
 SUB = 256
 VMEM_LIMIT = 56 * 1024 * 1024
 MESH = pl.DeviceIdType.MESH
@@ -150,12 +150,39 @@
     return hi, (x - hi.astype(jnp.float32)).astype(jnp.bfloat16)
 
 
-def factor_kernel(
-    rows_here, width, fac_width, piv_ref, all_ref, out_ref, hi_ref, lo_ref, side_ref, work
+def main_kernel(
+    n_cols, piv_ref, all_ref, solved_ref, emb_ref, fac_ref,
+    new_ref, gain_ref, best_ref,
+    emb_buf, fac_buf, hi_buf, lo_buf, new_buf, piv_buf, work, in_sem, out_sem,
 ):
+    f32, bf16 = jnp.float32, jnp.bfloat16
+    rows_here, width = emb_ref.shape
+    fac_width = fac_ref.shape[1]
     total = piv_ref.shape[1]
     slots = all_ref.shape[0]
-    f32 = jnp.float32
+    chunks = rows_here // SUB
+    blocks = total // GROUP
+    first = (lax.axis_index("rows") * n_cols + lax.axis_index("cols")) * rows_here
+
+    def at(c):
+        return pl.ds(pl.multiple_of(c * SUB, SUB), SUB)
+
+    def loads(c):
+        return (
+            pltpu.make_async_copy(emb_ref.at[at(c), :], emb_buf.at[at(c), :], in_sem.at[0, c]),
+            pltpu.make_async_copy(fac_ref.at[at(c), :], fac_buf.at[at(c), :], in_sem.at[1, c]),
+        )
+
+    def store(c):
+        return pltpu.make_async_copy(new_buf.at[at(c), :], new_ref.at[at(c), :], out_sem.at[c])
+
+    def start_loads(c, carry):
+        for copy in loads(c):
+            copy.start()
+        return carry
+
+    lax.fori_loop(0, chunks, start_loads, 0)
+
     sub = lax.broadcasted_iota(jnp.int32, (total, total), 0)
     lane = lax.broadcasted_iota(jnp.int32, (total, total), 1)
     eye = sub == lane
@@ -169,17 +196,17 @@
     before = total - jnp.sum(jnp.where(above, 1.0, 0.0), axis=0, keepdims=True)
     rank = place.astype(f32) - before
     chosen = above & (ids < low + rows_here) & (rank == (slot - owner * PMAX).astype(f32))
-    chosen = jnp.where(chosen, 1.0, 0.0).astype(jnp.bfloat16)
+    chosen = jnp.where(chosen, 1.0, 0.0).astype(bf16)
     full_width = all_ref.shape[1]
     part = width // 2
     for start in range(0, full_width, part):
         size = min(part, full_width - start)
-        out_ref[:, start:start + size] = jnp.dot(
+        piv_buf[:, start:start + size] = jnp.dot(
             chosen, all_ref[:, start:start + size], preferred_element_type=f32
-        ).astype(jnp.bfloat16)
-    emb = out_ref[:, :width]
-    fac = out_ref[:, width:width + fac_width]
-    count = out_ref[:, width + fac_width:width + fac_width + 1].astype(f32)
+        ).astype(bf16)
+    emb = piv_buf[:, :width]
+    fac = piv_buf[:, width:width + fac_width]
+    count = piv_buf[:, width + fac_width:width + fac_width + 1].astype(f32)
     wide = emb.astype(f32)
     norm = lax.rsqrt(jnp.sum(wide * wide, axis=1, keepdims=True) / width + EPS)
     q = learn(count)
@@ -187,126 +214,148 @@
     def to_row(col):
         return jnp.sum(jnp.where(eye, col, 0.0), axis=0, keepdims=True)
 
-    norm_row = to_row(norm) * (TAU / width)
+    norm_row = to_row(norm) * (TAU * LOG2E / width)
     q_row = to_row(q)
-    side_ref[0:1, :] = norm_row
-    side_ref[1:2, :] = q_row
     dots = lax.dot_general(emb, emb, NT, preferred_element_type=f32)
     shared = lax.dot_general(fac, fac, NT, preferred_element_type=f32)
-    block = q * q_row * jnp.exp(dots * norm * norm_row - TAU) - shared
-    work[...] = block + jnp.where(eye, RIDGE, 0.0)
+    block = q * q_row * jnp.exp2(dots * norm * norm_row - TAU * LOG2E) - shared
+    block = block + jnp.where(eye, RIDGE, 0.0)
+    work[...] = block
 
     row8 = lax.broadcasted_iota(jnp.int32, (GROUP, total), 0)
     lane8 = lax.broadcasted_iota(jnp.int32, (GROUP, total), 1)
 
-    def step(b, carry):
+    def column(rows, j):
+        col = jnp.sum(jnp.where(lane8 == j, rows, 0.0), axis=1, keepdims=True)
+        return jnp.broadcast_to(col, (GROUP, total))
+
+    def factor_step(b, carry):
+        rows, left, before = carry
         start = pl.multiple_of(b * GROUP, GROUP)
-        rows = work[pl.ds(start, GROUP), :]
-        cols = [
-            jnp.broadcast_to(
-                jnp.sum(jnp.where(lane8 == start + i, rows, 0.0), axis=1, keepdims=True),
-                (GROUP, total),
-            )
-            for i in range(GROUP)
-        ]
-        left = jnp.where(lane8 >= start + GROUP, rows, 0.0)
-        solved = jnp.where(
-            (lane8 >= start) & (lane8 < start + GROUP),
-            jnp.where(lane8 == start + row8, 1.0, 0.0),
-            rows,
+        cols = [column(rows, start + i) for i in range(GROUP)]
+        inside = (lane8 >= start) & (lane8 < start + GROUP)
+        mine = jnp.where(inside, jnp.where(lane8 == start + row8, 1.0, 0.0), rows)
+        delta = lax.dot_general(
+            left, before, (((0,), (0,)), ((), ())),
+            precision=lax.Precision.HIGHEST, preferred_element_type=f32,
         )
+        keep = jnp.where((lane >= start - GROUP) & (lane < start), 0.0, work[...])
+        work[...] = keep - delta
+        work[pl.ds(pl.multiple_of(jnp.maximum(start - GROUP, 0), GROUP), GROUP), :] = before
+        later = pl.multiple_of(jnp.minimum(start + GROUP, total - GROUP), GROUP)
+        ahead = work[pl.ds(later, GROUP), :]
+        acols = [column(ahead, start + i) for i in range(GROUP)]
+        ahead = jnp.where(inside, 0.0, ahead)
         diag = jnp.ones((GROUP, total), f32)
         for i in range(GROUP):
             d = cols[i][i:i + 1, :]
             diag = jnp.where(row8 == i, d, diag)
-            m = jnp.where(row8 > i, cols[i] * (1.0 / d), 0.0)
+            r = 1.0 / d
+            m = jnp.where(row8 > i, cols[i] * r, 0.0)
+            am = acols[i] * r
             for n in range(i + 1, GROUP):
-                cols[n] = cols[n] - m * cols[n][i:i + 1, :]
-            solved = solved - m * solved[i:i + 1, :]
-            left = left - m * left[i:i + 1, :]
-        scale = lax.rsqrt(diag)
-        solved = solved * scale
-        left = left * scale
-        delta = lax.dot_general(
-            left, solved, (((0,), (0,)), ((), ())),
-            precision=lax.Precision.HIGHEST, preferred_element_type=f32,
+                top = cols[n][i:i + 1, :]
+                cols[n] = cols[n] - m * top
+                acols[n] = acols[n] - am * top
+            top = mine[i:i + 1, :]
+            mine = mine - m * top
+            ahead = ahead - am * top
+        mine = mine * lax.rsqrt(diag)
+        left = jnp.where(lane8 >= start + GROUP, mine, 0.0)
+        return ahead, left, mine
+
+    wide_sub = lax.broadcasted_iota(jnp.int32, (LANES, LANES), 0)
+    wide_lane = lax.broadcasted_iota(jnp.int32, (LANES, LANES), 1)
+    small_eye = wide_sub == wide_lane
+    ones = jnp.ones((2 * LANES, LANES), bf16)
+    row = lax.broadcasted_iota(jnp.int32, (SUB, total), 0)
+    here = piv_ref[...] - first
+
+    def lane_sum(x):
+        x = x.astype(f32)
+        x = x * x
+        acc = x[:, :LANES]
+        for k in range(LANES, x.shape[1], LANES):
+            acc = acc + x[:, k:k + LANES]
+        hi, lo = split(acc)
+        return jnp.dot(jnp.concatenate([hi, lo], axis=1), ones, preferred_element_type=f32)
+
+    def spread(x):
+        return jnp.concatenate([x] * (total // LANES), axis=1)
+
+    def lines(x):
+        return [
+            jnp.sum(jnp.where(small_eye, x[g:g + LANES, :], 0.0), axis=0, keepdims=True)
+            for g in range(0, SUB, LANES)
+        ]
+
+    def panel_step(c):
+        for copy in loads(c):
+            copy.wait()
+        emb = emb_buf[at(c), :]
+        fac = fac_buf[at(c), :]
+        dots = lax.dot_general(emb, piv_buf[:, :width], NT, preferred_element_type=f32)
+        shared = lax.dot_general(
+            fac, piv_buf[:, width:width + fac_width], NT, preferred_element_type=f32
         )
-        keep = jnp.where((lane >= start) & (lane < start + GROUP), 0.0, work[...])
-        work[...] = keep - delta
-        work[pl.ds(start, GROUP), :] = solved
+        norm = lax.rsqrt(lane_sum(emb) / width + EPS)
+        used = lane_sum(fac)
+        counts = [
+            jnp.where(small_eye, solved_ref[pl.ds(c * (SUB // LANES) + g, 1), :].astype(f32), 0.0)
+            for g in range(SUB // LANES)
+        ]
+        counts = jnp.concatenate(counts, axis=0).astype(bf16)
+        q = learn(jnp.dot(counts, ones[:LANES, :], preferred_element_type=f32))
+        panel = spread(q) * q_row * jnp.exp2(dots * spread(norm) * norm_row - TAU * LOG2E) - shared
+        panel = jnp.where(row == here - c * SUB, panel + RIDGE, panel)
+        hi, lo = split(panel)
+        hi_buf[at(c), :] = hi
+        lo_buf[at(c), :] = lo
+        for g, line in enumerate(lines(q * q + RIDGE - used)):
+            gain_ref[pl.ds(c * (SUB // LANES) + g, 1), :] = line
+
+    def both(b, carry):
+        carry = factor_step(b, carry)
+        panel_step(b)
         return carry
 
-    lax.fori_loop(0, total // GROUP, step, 0)
-    hi, lo = split(work[...])
-    hi_ref[...] = hi
-    lo_ref[...] = lo
-
-
-def panel_kernel(
-    n_cols, rows_here, width, fac_width,
-    emb_ref, fac_ref, solved_ref, piv_ref, ids_ref, hi_ref, lo_ref, side_ref,
-    new_ref, gain_ref, best_ref,
-):
-    f32 = jnp.float32
-    total = ids_ref.shape[1]
-    tile = emb_ref.shape[0]
-    step = pl.program_id(0)
-    first = (lax.axis_index("rows") * n_cols + lax.axis_index("cols")) * rows_here + step * tile
-    piv_emb = piv_ref[:, :width]
-    piv_fac = piv_ref[:, width:width + fac_width]
-    hi_w = hi_ref[...]
-    lo_w = lo_ref[...]
-    norm_row = side_ref[0:1, :]
-    q_row = side_ref[1:2, :]
-    ids = ids_ref[...] - first
-    sub = lax.broadcasted_iota(jnp.int32, (LANES, LANES), 0)
-    lane = lax.broadcasted_iota(jnp.int32, (LANES, LANES), 1)
-    eye = sub == lane
-    row = lax.broadcasted_iota(jnp.int32, (SUB, total), 0)
-    q_lanes = learn(solved_ref[...])
-    best = jnp.full((1, LANES), -jnp.inf, f32)
-    for s in range(0, tile, SUB):
-        emb = emb_ref[s:s + SUB, :]
-        fac = fac_ref[s:s + SUB, :]
-        dots = lax.dot_general(emb, piv_emb, NT, preferred_element_type=f32)
-        shared = lax.dot_general(fac, piv_fac, NT, preferred_element_type=f32)
-        wide = emb.astype(f32)
-        norm = lax.rsqrt(jnp.sum(wide * wide, axis=1, keepdims=True) / width + EPS)
-        widef = fac.astype(f32)
-        used = jnp.sum(widef * widef, axis=1, keepdims=True)
-        q = jnp.concatenate(
-            [
-                jnp.sum(
-                    jnp.where(eye, q_lanes[g:g + 1, :], 0.0), axis=1, keepdims=True
-                )
-                for g in range(s // LANES, (s + SUB) // LANES)
-            ],
-            axis=0,
-        )
-        panel = q * q_row * jnp.exp(dots * norm * norm_row - TAU) - shared
-        panel = jnp.where(row + s == ids, panel + RIDGE, panel)
-        hi, lo = split(panel)
+    def panel_only(c, carry):
+        panel_step(c)
+        return carry
+
+    shared_steps = min(blocks, chunks)
+    zero = jnp.zeros((GROUP, total), f32)
+    carry = lax.fori_loop(0, shared_steps, both, (block[:GROUP, :], zero, zero))
+    carry = lax.fori_loop(shared_steps, blocks, factor_step, carry)
+    lax.fori_loop(shared_steps, chunks, panel_only, 0)
+    work[total - GROUP:, :] = carry[2]
+    hi_w, lo_w = split(jnp.where(lane <= sub, work[...], 0.0))
+
+    def solve_step(c, best):
+        hi = hi_buf[at(c), :]
+        lo = lo_buf[at(c), :]
         full = (
             lax.dot_general(hi, hi_w, NT, preferred_element_type=f32)
             + lax.dot_general(hi, lo_w, NT, preferred_element_type=f32)
             + lax.dot_general(lo, hi_w, NT, preferred_element_type=f32)
         )
-        new_ref[s:s + SUB, :] = full.astype(jnp.bfloat16)
-        gain = q * q + RIDGE - used - jnp.sum(full * full, axis=1, keepdims=True)
-        for g in range(0, SUB, LANES):
-            line = jnp.sum(jnp.where(eye, gain[g:g + LANES, :], 0.0), axis=0, keepdims=True)
-            at = (s + g) // LANES
-            gain_ref[at:at + 1, :] = line
-            best = jnp.maximum(best, line)
-    best = jnp.broadcast_to(best, best_ref.shape)
-
-    @pl.when(step == 0)
-    def _():
-        best_ref[...] = best
-
-    @pl.when(step > 0)
-    def _():
-        best_ref[...] = jnp.maximum(best_ref[...], best)
+        new_buf[at(c), :] = full.astype(bf16)
+        store(c).start()
+        for g, line in enumerate(lines(lane_sum(full))):
+            where = pl.ds(c * (SUB // LANES) + g, 1)
+            gain = gain_ref[where, :] - line
+            gain_ref[where, :] = gain
+            best = jnp.maximum(best, gain)
+        return best
+
+    best = lax.fori_loop(0, chunks, solve_step, jnp.full((1, LANES), -jnp.inf, f32))
+    best_ref[...] = jnp.broadcast_to(best, best_ref.shape)
+
+    def finish(c, carry):
+        store(c).wait()
+        return carry
+
+    lax.fori_loop(0, chunks, finish, 0)
 
 
 def best_kernel(n_rows, n_cols, own_ref, out_ref, stage, buf_r, buf_c, send_r, recv_r, send_c, recv_c):
@@ -376,53 +425,35 @@
         compiler_params=params(collective_id=0, has_side_effects=True),
         name="gather",
     )(own)
-    ids = pivots.reshape(1, total)
-    piv, hi, lo, side = pl.pallas_call(
-        functools.partial(factor_kernel, rows_here, width, fac_width),
-        out_shape=[
-            jax.ShapeDtypeStruct((total, packet), bf16),
-            jax.ShapeDtypeStruct((total, total), bf16),
-            jax.ShapeDtypeStruct((total, total), bf16),
-            jax.ShapeDtypeStruct((8, total), jnp.float32),
-        ],
-        in_specs=[vmem, vmem],
-        out_specs=[vmem] * 4,
-        scratch_shapes=[pltpu.VMEM((total, total), jnp.float32)],
-        compiler_params=params(),
-        name="factor",
-    )(ids, everyone.reshape(devices * PMAX, packet))
-    tile = TILE
     lines = rows_here // LANES
-
-    def whole(shape):
-        return pl.BlockSpec(shape, lambda t: (0, 0))
-
+    hbm = pl.BlockSpec(memory_space=pl.ANY)
+    chunks = rows_here // SUB
     new_cols, gains, best = pl.pallas_call(
-        functools.partial(panel_kernel, n_cols, rows_here, width, fac_width),
+        functools.partial(main_kernel, n_cols),
         out_shape=[
             jax.ShapeDtypeStruct((rows_here, total), bf16),
             jax.ShapeDtypeStruct((lines, LANES), jnp.float32),
             jax.ShapeDtypeStruct((8, LANES), jnp.float32),
         ],
-        grid=(rows_here // tile,),
-        in_specs=[
-            pl.BlockSpec((tile, width), lambda t: (t, 0)),
-            pl.BlockSpec((tile, fac_width), lambda t: (t, 0)),
-            pl.BlockSpec((tile // LANES, LANES), lambda t: (t, 0)),
-            whole((total, packet)),
-            whole((1, total)),
-            whole((total, total)),
-            whole((total, total)),
-            whole((8, total)),
-        ],
-        out_specs=[
-            pl.BlockSpec((tile, total), lambda t: (t, 0)),
-            pl.BlockSpec((tile // LANES, LANES), lambda t: (t, 0)),
-            whole((8, LANES)),
+        in_specs=[vmem, vmem, vmem, hbm, hbm],
+        out_specs=[hbm, vmem, vmem],
+        scratch_shapes=[
+            pltpu.VMEM((rows_here, width), bf16),
+            pltpu.VMEM((rows_here, fac_width), bf16),
+            pltpu.VMEM((rows_here, total), bf16),
+            pltpu.VMEM((rows_here, total), bf16),
+            pltpu.VMEM((rows_here, total), bf16),
+            pltpu.VMEM((total, packet), bf16),
+            pltpu.VMEM((total, total), jnp.float32),
+            pltpu.SemaphoreType.DMA((2, chunks)),
+            pltpu.SemaphoreType.DMA((chunks,)),
         ],
         compiler_params=params(),
-        name="panel",
-    )(embeddings, factor_cols, solved.reshape(lines, LANES), piv, ids, hi, lo, side)
+        name="main",
+    )(
+        pivots.reshape(1, total), everyone.reshape(devices * PMAX, packet),
+        solved.reshape(lines, LANES), embeddings, factor_cols,
+    )
     top = pl.pallas_call(
         functools.partial(best_kernel, n_rows, n_cols),
         out_shape=jax.ShapeDtypeStruct((1, 1), jnp.float32),

time: 82.3 us -> 97.8 us (1.19)
  Pallas kernels: 79.7 us -> 95 us
    pallas_call x2 -> x1, Pallas kernels: 43.4 us -> 58.8 us  [body(): pl.pallas_call(functools.partial(main_kernel, n_cols), out_shape=[jax.Sha...]
where the time goes in v2:
time: 97.8 us; the launch traced here: 97.4 us
  Pallas kernels  95 us (97%)
  between operations  2.34 us (2%)
    pallas_call x1, Pallas kernels, body(): pl.pallas_call(functools.partial(main_kernel, n_cols), out_shape=[jax.Sha...  58.8 us
    pallas_call x1, Pallas kernels, body(): pl.pallas_call(functools.partial(gather_kernel, n_rows, n_cols), out_shap...  22.3 us
    pallas_call x1, Pallas kernels, body(): pl.pallas_call(functools.partial(best_kernel, n_rows, n_cols), out_shape=...  10.2 us
    pallas_call x1, Pallas kernels, body(): pl.pallas_call(functools.partial(pick_kernel, n_cols), out_shape=jax.Shap...  3.75 us

profile of v2, /device:TPU:0, one launch (start us, length us, event | category | flops | bytes accessed | tf_op | source)
XLA Modules:
  0.0 97.4 jit_solution(13679999296305779138)
XLA Ops:
  0.6 3.8 %pick.1.own_ref = bf16[16,1664]{1,0:T(8,128)(2,1)} custom-call(s32[256]{0:T(256)} %piv_ref.1, s32[7168]{0:T(1024)} %solved_ref.1, bf16[7168,1024]{1,0:T(8,128)(2,1)} %emb_ref.3, bf16[7168,512]{1,0:T(8,128)(2,1)} %fac_ref.3), custom_call_target="tpu_custom_call" | custom-call | tf_op jit(solution)/shard_map/pick/pallas_call | solution.py:402
  4.4 22.3 %gather.1 = bf16[32,16,1664]{2,1,0:T(8,128)(2,1)} custom-call(bf16[16,1664]{1,0:T(8,128)(2,1)} %pick.1.own_ref), custom_call_target="tpu_custom_call" | custom-call | tf_op jit(solution)/shard_map/gather/pallas_call | solution.py:415
  26.7 58.8 %main.1 = (bf16[7168,256]{1,0:T(8,128)(2,1)}, f32[56,128]{1,0:T(8,128)}, f32[8,128]{1,0:T(8,128)}) custom-call(s32[1,256]{1,0:T(1,128)} %bitcast.7, bf16[512,1664]{1,0:T(8,128)(2,1)} %bitcast.5, s32[56,128]{1,0:T(8,128)} %bitcast.6, bf16[7168,1024]{1,0:T(8,128)(2,1)} %emb_ref.3, bf16[7168,512]{1,0:T(8,128)(2,1)} %fac_ref.3), custom_call_target="tpu_custom_call" | custom-call | tf_op jit(solution)/shard_map/main/pallas_call | solution.py:431
  85.5 10.2 %best.1 = f32[1,1]{1,0:T(1,128)} custom-call(f32[8,128]{1,0:T(8,128)} %get-tuple-element.8.own_ref), custom_call_target="tpu_custom_call" | custom-call | tf_op jit(solution)/shard_map/best/pallas_call | solution.py:457

commit v3 on v2

--- a/solution.py
+++ b/solution.py
@@ -153,7 +153,7 @@
 def main_kernel(
     n_cols, piv_ref, all_ref, solved_ref, emb_ref, fac_ref,
     new_ref, gain_ref, best_ref,
-    emb_buf, fac_buf, hi_buf, lo_buf, new_buf, piv_buf, work, in_sem, out_sem,
+    emb_buf, fac_buf, hi_buf, lo_buf, new_buf, piv_buf, turn_buf, work, in_sem, out_sem,
 ):
     f32, bf16 = jnp.float32, jnp.bfloat16
     rows_here, width = emb_ref.shape
@@ -216,8 +216,13 @@
 
     norm_row = to_row(norm) * (TAU * LOG2E / width)
     q_row = to_row(q)
-    dots = lax.dot_general(emb, emb, NT, preferred_element_type=f32)
-    shared = lax.dot_general(fac, fac, NT, preferred_element_type=f32)
+    used_width = width + fac_width
+    for start in range(0, used_width, LANES):
+        turn_buf[start:start + LANES, :] = (
+            piv_buf[:, start:start + LANES].astype(f32).T.astype(bf16)
+        )
+    dots = jnp.dot(emb, turn_buf[:width, :], preferred_element_type=f32)
+    shared = jnp.dot(fac, turn_buf[width:, :], preferred_element_type=f32)
     block = q * q_row * jnp.exp2(dots * norm * norm_row - TAU * LOG2E) - shared
     block = block + jnp.where(eye, RIDGE, 0.0)
     work[...] = block
@@ -294,10 +299,8 @@
             copy.wait()
         emb = emb_buf[at(c), :]
         fac = fac_buf[at(c), :]
-        dots = lax.dot_general(emb, piv_buf[:, :width], NT, preferred_element_type=f32)
-        shared = lax.dot_general(
-            fac, piv_buf[:, width:width + fac_width], NT, preferred_element_type=f32
-        )
+        dots = jnp.dot(emb, turn_buf[:width, :], preferred_element_type=f32)
+        shared = jnp.dot(fac, turn_buf[width:, :], preferred_element_type=f32)
         norm = lax.rsqrt(lane_sum(emb) / width + EPS)
         used = lane_sum(fac)
         counts = [
@@ -329,15 +332,14 @@
     carry = lax.fori_loop(shared_steps, blocks, factor_step, carry)
     lax.fori_loop(shared_steps, chunks, panel_only, 0)
     work[total - GROUP:, :] = carry[2]
-    hi_w, lo_w = split(jnp.where(lane <= sub, work[...], 0.0))
+    hi_w, lo_w = split(jnp.where(lane <= sub, work[...], 0.0).T)
+    triple = jnp.concatenate([hi_w, lo_w, hi_w], axis=0)
 
     def solve_step(c, best):
         hi = hi_buf[at(c), :]
         lo = lo_buf[at(c), :]
-        full = (
-            lax.dot_general(hi, hi_w, NT, preferred_element_type=f32)
-            + lax.dot_general(hi, lo_w, NT, preferred_element_type=f32)
-            + lax.dot_general(lo, hi_w, NT, preferred_element_type=f32)
+        full = jnp.dot(
+            jnp.concatenate([hi, hi, lo], axis=1), triple, preferred_element_type=f32
         )
         new_buf[at(c), :] = full.astype(bf16)
         store(c).start()
@@ -358,35 +360,32 @@
     lax.fori_loop(0, chunks, finish, 0)
 
 
-def best_kernel(n_rows, n_cols, own_ref, out_ref, stage, buf_r, buf_c, send_r, recv_r, send_c, recv_c):
+def best_kernel(n_rows, n_cols, own_ref, out_ref, buf, send_sem, recv_sem):
     r = lax.axis_index("rows")
     c = lax.axis_index("cols")
+    peers = [
+        (lax.rem(r + j, n_rows), lax.rem(c + i, n_cols))
+        for j in range(n_rows) for i in range(n_cols) if i or j
+    ]
     barrier = pltpu.get_barrier_semaphore()
-    peers_r = [(lax.rem(r + j, n_rows), c) for j in range(1, n_rows)]
-    peers_c = [(r, lax.rem(c + i, n_cols)) for i in range(1, n_cols)]
-    for peer in peers_r + peers_c:
+    for peer in peers:
         pl.semaphore_signal(barrier, inc=1, device_id=peer, device_id_type=MESH)
-    pl.semaphore_wait(barrier, len(peers_r) + len(peers_c))
-
-    def exchange(src, buf, send_sem, recv_sem, peers):
-        copies = []
-        for j, peer in enumerate(peers):
-            copy = pltpu.make_async_remote_copy(
-                src_ref=src, dst_ref=buf.at[j], send_sem=send_sem.at[j],
-                recv_sem=recv_sem.at[j], device_id=peer, device_id_type=MESH,
-            )
-            copy.start()
-            copies.append(copy)
-        top = src[...]
-        for j, copy in enumerate(copies):
-            copy.wait_recv()
-            top = jnp.maximum(top, buf[j])
-        for copy in copies:
-            copy.wait_send()
-        return top
-
-    stage[...] = exchange(own_ref, buf_r, send_r, recv_r, peers_r)
-    out_ref[0, 0] = jnp.max(exchange(stage, buf_c, send_c, recv_c, peers_c))
+    pl.semaphore_wait(barrier, len(peers))
+    copies = []
+    for j, peer in enumerate(peers):
+        copy = pltpu.make_async_remote_copy(
+            src_ref=own_ref, dst_ref=buf.at[j], send_sem=send_sem.at[j],
+            recv_sem=recv_sem.at[j], device_id=peer, device_id_type=MESH,
+        )
+        copy.start()
+        copies.append(copy)
+    top = own_ref[...]
+    for j, copy in enumerate(copies):
+        copy.wait_recv()
+        top = jnp.maximum(top, buf[j])
+    out_ref[0, 0] = jnp.max(top)
+    for copy in copies:
+        copy.wait_send()
 
 
 def body(n_rows, n_cols, embeddings, factor_cols, solved, pivots):
@@ -444,6 +443,7 @@
             pltpu.VMEM((rows_here, total), bf16),
             pltpu.VMEM((rows_here, total), bf16),
             pltpu.VMEM((total, packet), bf16),
+            pltpu.VMEM((width + fac_width, total), bf16),
             pltpu.VMEM((total, total), jnp.float32),
             pltpu.SemaphoreType.DMA((2, chunks)),
             pltpu.SemaphoreType.DMA((chunks,)),
@@ -460,13 +460,9 @@
         in_specs=[vmem],
         out_specs=smem,
         scratch_shapes=[
-            pltpu.VMEM((8, LANES), jnp.float32),
-            pltpu.VMEM((n_rows, 8, LANES), jnp.float32),
-            pltpu.VMEM((n_cols, 8, LANES), jnp.float32),
-            pltpu.SemaphoreType.DMA((n_rows,)),
-            pltpu.SemaphoreType.DMA((n_rows,)),
-            pltpu.SemaphoreType.DMA((n_cols,)),
-            pltpu.SemaphoreType.DMA((n_cols,)),
+            pltpu.VMEM((devices - 1, 8, LANES), jnp.float32),
+            pltpu.SemaphoreType.DMA((devices - 1,)),
+            pltpu.SemaphoreType.DMA((devices - 1,)),
         ],
         compiler_params=params(collective_id=1, has_side_effects=True),
         name="best",

time: 97.8 us -> 95.9 us (0.981)
  Pallas kernels: 95 us -> 93.2 us
    pallas_call x1, Pallas kernels: 58.8 us -> 57.1 us  [body(): pl.pallas_call(functools.partial(main_kernel, n_cols), out_shape=[jax.Sha...]
where the time goes in v3:
time: 95.9 us; the launch traced here: 95.5 us
  Pallas kernels  93.2 us (97%)
  between operations  2.34 us (2%)
    pallas_call x1, Pallas kernels, body(): pl.pallas_call(functools.partial(main_kernel, n_cols), out_shape=[jax.Sha...  57.1 us
    pallas_call x1, Pallas kernels, body(): pl.pallas_call(functools.partial(gather_kernel, n_rows, n_cols), out_shap...  22.5 us
    pallas_call x1, Pallas kernels, body(): pl.pallas_call(functools.partial(best_kernel, n_rows, n_cols), out_shape=...  9.95 us
    pallas_call x1, Pallas kernels, body(): pl.pallas_call(functools.partial(pick_kernel, n_cols), out_shape=jax.Shap...  3.63 us

profile of v3, /device:TPU:0, one launch (start us, length us, event | category | flops | bytes accessed | tf_op | source)
XLA Modules:
  0.0 95.5 jit_solution(15615736539437242265)
XLA Ops:
  0.6 3.6 %pick.1.own_ref = bf16[16,1664]{1,0:T(8,128)(2,1)} custom-call(s32[256]{0:T(256)} %piv_ref.1, s32[7168]{0:T(1024)} %solved_ref.1, bf16[7168,1024]{1,0:T(8,128)(2,1)} %emb_ref.3, bf16[7168,512]{1,0:T(8,128)(2,1)} %fac_ref.3), custom_call_target="tpu_custom_call" | custom-call | tf_op jit(solution)/shard_map/pick/pallas_call | solution.py:401
  4.3 22.5 %gather.1 = bf16[32,16,1664]{2,1,0:T(8,128)(2,1)} custom-call(bf16[16,1664]{1,0:T(8,128)(2,1)} %pick.1.own_ref), custom_call_target="tpu_custom_call" | custom-call | tf_op jit(solution)/shard_map/gather/pallas_call | solution.py:414
  26.8 57.1 %main.1 = (bf16[7168,256]{1,0:T(8,128)(2,1)}, f32[56,128]{1,0:T(8,128)}, f32[8,128]{1,0:T(8,128)}) custom-call(s32[1,256]{1,0:T(1,128)} %bitcast.7, bf16[512,1664]{1,0:T(8,128)(2,1)} %bitcast.5, s32[56,128]{1,0:T(8,128)} %bitcast.6, bf16[7168,1024]{1,0:T(8,128)(2,1)} %emb_ref.3, bf16[7168,512]{1,0:T(8,128)(2,1)} %fac_ref.3), custom_call_target="tpu_custom_call" | custom-call | tf_op jit(solution)/shard_map/main/pallas_call | solution.py:430
  83.9 10.0 %best.1 = f32[1,1]{1,0:T(1,128)} custom-call(f32[8,128]{1,0:T(8,128)} %get-tuple-element.8.own_ref), custom_call_target="tpu_custom_call" | custom-call | tf_op jit(solution)/shard_map/best/pallas_call | solution.py:457

commit v4 on v3

--- a/solution.py
+++ b/solution.py
@@ -15,6 +15,7 @@
 LANES = 128
 GROUP = 8
 SUB = 256
+PIECE = 32
 VMEM_LIMIT = 56 * 1024 * 1024
 MESH = pl.DeviceIdType.MESH
 NT = (((1,), (1,)), ((), ()))
@@ -153,7 +154,8 @@
 def main_kernel(
     n_cols, piv_ref, all_ref, solved_ref, emb_ref, fac_ref,
     new_ref, gain_ref, best_ref,
-    emb_buf, fac_buf, hi_buf, lo_buf, new_buf, piv_buf, turn_buf, work, in_sem, out_sem,
+    emb_buf, fac_buf, hi_buf, lo_buf, new_buf, piv_buf, turn_buf, work, delta_buf, dots_buf, shared_buf, stat_buf, sum_buf,
+    in_sem, out_sem,
 ):
     f32, bf16 = jnp.float32, jnp.bfloat16
     rows_here, width = emb_ref.shape
@@ -230,6 +232,9 @@
     row8 = lax.broadcasted_iota(jnp.int32, (GROUP, total), 0)
     lane8 = lax.broadcasted_iota(jnp.int32, (GROUP, total), 1)
 
+    lane_piece = lax.broadcasted_iota(jnp.int32, (PIECE, total), 1)
+    row_piece = lax.broadcasted_iota(jnp.int32, (PIECE, total), 0)
+
     def column(rows, j):
         col = jnp.sum(jnp.where(lane8 == j, rows, 0.0), axis=1, keepdims=True)
         return jnp.broadcast_to(col, (GROUP, total))
@@ -244,8 +249,12 @@
             left, before, (((0,), (0,)), ((), ())),
             precision=lax.Precision.HIGHEST, preferred_element_type=f32,
         )
-        keep = jnp.where((lane >= start - GROUP) & (lane < start), 0.0, work[...])
-        work[...] = keep - delta
+        delta_buf[...] = delta
+        gone = (lane_piece >= start - GROUP) & (lane_piece < start)
+        for p in range(0, total, PIECE):
+            work[p:p + PIECE, :] = (
+                jnp.where(gone, 0.0, work[p:p + PIECE, :]) - delta_buf[p:p + PIECE, :]
+            )
         work[pl.ds(pl.multiple_of(jnp.maximum(start - GROUP, 0), GROUP), GROUP), :] = before
         later = pl.multiple_of(jnp.minimum(start + GROUP, total - GROUP), GROUP)
         ahead = work[pl.ds(later, GROUP), :]
@@ -273,48 +282,67 @@
     wide_lane = lax.broadcasted_iota(jnp.int32, (LANES, LANES), 1)
     small_eye = wide_sub == wide_lane
     ones = jnp.ones((2 * LANES, LANES), bf16)
-    row = lax.broadcasted_iota(jnp.int32, (SUB, total), 0)
+    eye_row = lax.broadcasted_iota(jnp.int32, (PIECE, LANES), 0)
+    eye_lane = lax.broadcasted_iota(jnp.int32, (PIECE, LANES), 1)
     here = piv_ref[...] - first
 
-    def lane_sum(x):
-        x = x.astype(f32)
-        x = x * x
-        acc = x[:, :LANES]
-        for k in range(LANES, x.shape[1], LANES):
-            acc = acc + x[:, k:k + LANES]
+    def squares(load, width, p, k):
+        acc = jnp.zeros((PIECE, LANES), f32)
+        for j in range(0, width, LANES):
+            x = load(j).astype(f32)
+            acc = acc + x * x
         hi, lo = split(acc)
-        return jnp.dot(jnp.concatenate([hi, lo], axis=1), ones, preferred_element_type=f32)
-
-    def spread(x):
-        return jnp.concatenate([x] * (total // LANES), axis=1)
-
-    def lines(x):
-        return [
-            jnp.sum(jnp.where(small_eye, x[g:g + LANES, :], 0.0), axis=0, keepdims=True)
-            for g in range(0, SUB, LANES)
-        ]
+        stat_buf[p:p + PIECE, k:k + LANES] = hi
+        stat_buf[p:p + PIECE, k + LANES:k + 2 * LANES] = lo
+
+    def row_sums(rows, k):
+        return jnp.dot(stat_buf[:rows, k:k + 2 * LANES], ones, preferred_element_type=f32)
+
+    def line_part(x, p):
+        mine = eye_lane == eye_row + p % LANES
+        return jnp.sum(jnp.where(mine, x, 0.0), axis=0, keepdims=True)
 
     def panel_step(c):
+        base = pl.multiple_of(c * SUB, SUB)
         for copy in loads(c):
             copy.wait()
-        emb = emb_buf[at(c), :]
-        fac = fac_buf[at(c), :]
-        dots = jnp.dot(emb, turn_buf[:width, :], preferred_element_type=f32)
-        shared = jnp.dot(fac, turn_buf[width:, :], preferred_element_type=f32)
-        norm = lax.rsqrt(lane_sum(emb) / width + EPS)
-        used = lane_sum(fac)
-        counts = [
-            jnp.where(small_eye, solved_ref[pl.ds(c * (SUB // LANES) + g, 1), :].astype(f32), 0.0)
-            for g in range(SUB // LANES)
-        ]
-        counts = jnp.concatenate(counts, axis=0).astype(bf16)
-        q = learn(jnp.dot(counts, ones[:LANES, :], preferred_element_type=f32))
-        panel = spread(q) * q_row * jnp.exp2(dots * spread(norm) * norm_row - TAU * LOG2E) - shared
-        panel = jnp.where(row == here - c * SUB, panel + RIDGE, panel)
-        hi, lo = split(panel)
-        hi_buf[at(c), :] = hi
-        lo_buf[at(c), :] = lo
-        for g, line in enumerate(lines(q * q + RIDGE - used)):
+        dots_buf[...] = jnp.dot(
+            emb_buf[at(c), :], turn_buf[:width, :], preferred_element_type=f32
+        )
+        shared_buf[...] = jnp.dot(
+            fac_buf[at(c), :], turn_buf[width:, :], preferred_element_type=f32
+        )
+        for p in range(0, SUB, PIECE):
+            rows = pl.ds(base + p, PIECE)
+            squares(lambda j: emb_buf[rows, j:j + LANES], width, p, 0)
+            squares(lambda j: fac_buf[rows, j:j + LANES], fac_width, p, 2 * LANES)
+        sum_buf[:SUB, :LANES] = row_sums(SUB, 0)
+        sum_buf[:SUB, LANES:2 * LANES] = row_sums(SUB, 2 * LANES)
+        for g in range(SUB // LANES):
+            line = solved_ref[pl.ds(c * (SUB // LANES) + g, 1), :].astype(f32)
+            counts = jnp.where(small_eye, line, 0.0).astype(bf16)
+            sum_buf[g * LANES:(g + 1) * LANES, 2 * LANES:] = jnp.dot(
+                counts, ones[:LANES, :], preferred_element_type=f32
+            )
+        for g in range(SUB // LANES):
+            line = jnp.zeros((1, LANES), f32)
+            for p in range(g * LANES, (g + 1) * LANES, PIECE):
+                rows = pl.ds(base + p, PIECE)
+                norm = lax.rsqrt(sum_buf[p:p + PIECE, :LANES] / width + EPS)
+                q = learn(sum_buf[p:p + PIECE, 2 * LANES:])
+                line = line + line_part(
+                    q * q + RIDGE - sum_buf[p:p + PIECE, LANES:2 * LANES], p
+                )
+                for k in range(0, total, LANES):
+                    half = slice(k, k + LANES)
+                    power = dots_buf[p:p + PIECE, half] * norm * norm_row[:, half] - TAU * LOG2E
+                    panel = q * q_row[:, half] * jnp.exp2(power) - shared_buf[p:p + PIECE, half]
+                    panel = jnp.where(
+                        row_piece[:, half] == here[:, half] - (base + p), panel + RIDGE, panel
+                    )
+                    hi, lo = split(panel)
+                    hi_buf[rows, half] = hi
+                    lo_buf[rows, half] = lo
             gain_ref[pl.ds(c * (SUB // LANES) + g, 1), :] = line
 
     def both(b, carry):
@@ -336,14 +364,20 @@
     triple = jnp.concatenate([hi_w, lo_w, hi_w], axis=0)
 
     def solve_step(c, best):
-        hi = hi_buf[at(c), :]
-        lo = lo_buf[at(c), :]
-        full = jnp.dot(
-            jnp.concatenate([hi, hi, lo], axis=1), triple, preferred_element_type=f32
-        )
-        new_buf[at(c), :] = full.astype(bf16)
+        base = pl.multiple_of(c * SUB, SUB)
+        dots_buf[...] = jnp.dot(
+            jnp.concatenate([hi_buf[at(c), :], hi_buf[at(c), :], lo_buf[at(c), :]], axis=1),
+            triple, preferred_element_type=f32,
+        )
+        for p in range(0, SUB, PIECE):
+            new_buf[pl.ds(base + p, PIECE), :] = dots_buf[p:p + PIECE, :].astype(bf16)
+            squares(lambda j: dots_buf[p:p + PIECE, j:j + LANES], total, p, 0)
         store(c).start()
-        for g, line in enumerate(lines(lane_sum(full))):
+        sum_buf[:SUB, :LANES] = row_sums(SUB, 0)
+        for g in range(SUB // LANES):
+            line = jnp.zeros((1, LANES), f32)
+            for p in range(g * LANES, (g + 1) * LANES, PIECE):
+                line = line + line_part(sum_buf[p:p + PIECE, :LANES], p)
             where = pl.ds(c * (SUB // LANES) + g, 1)
             gain = gain_ref[where, :] - line
             gain_ref[where, :] = gain
@@ -445,6 +479,11 @@
             pltpu.VMEM((total, packet), bf16),
             pltpu.VMEM((width + fac_width, total), bf16),
             pltpu.VMEM((total, total), jnp.float32),
+            pltpu.VMEM((total, total), jnp.float32),
+            pltpu.VMEM((SUB, total), jnp.float32),
+            pltpu.VMEM((SUB, total), jnp.float32),
+            pltpu.VMEM((SUB, 4 * LANES), bf16),
+            pltpu.VMEM((SUB, 3 * LANES), jnp.float32),
             pltpu.SemaphoreType.DMA((2, chunks)),
             pltpu.SemaphoreType.DMA((chunks,)),
         ],

time: 95.9 us -> 97.4 us (1.016)
  Pallas kernels: 93.2 us -> 94.4 us
    pallas_call x1, Pallas kernels: 57.1 us -> 58.7 us  [body(): pl.pallas_call(functools.partial(main_kernel, n_cols), out_shape=[jax.Sha...]
where the time goes in v4:
time: 97.4 us; the launch traced here: 96.8 us
  Pallas kernels  94.4 us (97%)
  between operations  2.34 us (2%)
    pallas_call x1, Pallas kernels, body(): pl.pallas_call(functools.partial(main_kernel, n_cols), out_shape=[jax.Sha...  58.7 us
    pallas_call x1, Pallas kernels, body(): pl.pallas_call(functools.partial(gather_kernel, n_rows, n_cols), out_shap...  22.1 us
    pallas_call x1, Pallas kernels, body(): pl.pallas_call(functools.partial(best_kernel, n_rows, n_cols), out_shape=...  9.95 us
    pallas_call x1, Pallas kernels, body(): pl.pallas_call(functools.partial(pick_kernel, n_cols), out_shape=jax.Shap...  3.74 us

profile of v4, /device:TPU:0, one launch (start us, length us, event | category | flops | bytes accessed | tf_op | source)
XLA Modules:
  0.0 96.8 jit_solution(16680683115455900304)
XLA Ops:
  0.6 3.7 %pick.1.own_ref = bf16[16,1664]{1,0:T(8,128)(2,1)} custom-call(s32[256]{0:T(256)} %piv_ref.1, s32[7168]{0:T(1024)} %solved_ref.1, bf16[7168,1024]{1,0:T(8,128)(2,1)} %emb_ref.3, bf16[7168,512]{1,0:T(8,128)(2,1)} %fac_ref.3), custom_call_target="tpu_custom_call" | custom-call | tf_op jit(solution)/shard_map/pick/pallas_call | solution.py:435
  4.4 22.1 %gather.1 = bf16[32,16,1664]{2,1,0:T(8,128)(2,1)} custom-call(bf16[16,1664]{1,0:T(8,128)(2,1)} %pick.1.own_ref), custom_call_target="tpu_custom_call" | custom-call | tf_op jit(solution)/shard_map/gather/pallas_call | solution.py:448
  26.4 58.7 %main.1 = (bf16[7168,256]{1,0:T(8,128)(2,1)}, f32[56,128]{1,0:T(8,128)}, f32[8,128]{1,0:T(8,128)}) custom-call(s32[1,256]{1,0:T(1,128)} %bitcast.7, bf16[512,1664]{1,0:T(8,128)(2,1)} %bitcast.5, s32[56,128]{1,0:T(8,128)} %bitcast.6, bf16[7168,1024]{1,0:T(8,128)(2,1)} %emb_ref.3, bf16[7168,512]{1,0:T(8,128)(2,1)} %fac_ref.3), custom_call_target="tpu_custom_call" | custom-call | tf_op jit(solution)/shard_map/main/pallas_call | solution.py:464
  85.1 10.0 %best.1 = f32[1,1]{1,0:T(1,128)} custom-call(f32[8,128]{1,0:T(8,128)} %get-tuple-element.8.own_ref), custom_call_target="tpu_custom_call" | custom-call | tf_op jit(solution)/shard_map/best/pallas_call | solution.py:496

commit v5 on v1

--- a/solution.py
+++ b/solution.py
@@ -11,10 +11,12 @@
 EPS = 1e-06
 TAU = 6.0
 RIDGE = 1.0
+LOG2E = 1.4426950408889634
 LANES = 128
 GROUP = 8
 TILE = 1024
 SUB = 256
+PIECE = 32
 VMEM_LIMIT = 56 * 1024 * 1024
 MESH = pl.DeviceIdType.MESH
 NT = (((1,), (1,)), ((), ()))
@@ -151,7 +153,7 @@
 
 
 def factor_kernel(
-    rows_here, width, fac_width, piv_ref, all_ref, out_ref, hi_ref, lo_ref, side_ref, work
+    rows_here, width, fac_width, piv_ref, all_ref, turn_ref, triple_ref, side_ref, out_ref, work
 ):
     total = piv_ref.shape[1]
     slots = all_ref.shape[0]
@@ -187,116 +189,174 @@
     def to_row(col):
         return jnp.sum(jnp.where(eye, col, 0.0), axis=0, keepdims=True)
 
-    norm_row = to_row(norm) * (TAU / width)
+    norm_row = to_row(norm) * (TAU * LOG2E / width)
     q_row = to_row(q)
     side_ref[0:1, :] = norm_row
     side_ref[1:2, :] = q_row
-    dots = lax.dot_general(emb, emb, NT, preferred_element_type=f32)
-    shared = lax.dot_general(fac, fac, NT, preferred_element_type=f32)
-    block = q * q_row * jnp.exp(dots * norm * norm_row - TAU) - shared
+    for start in range(0, width + fac_width, LANES):
+        turn_ref[start:start + LANES, :] = (
+            out_ref[:, start:start + LANES].astype(f32).T.astype(jnp.bfloat16)
+        )
+    dots = jnp.dot(emb, turn_ref[:width, :], preferred_element_type=f32)
+    shared = jnp.dot(fac, turn_ref[width:, :], preferred_element_type=f32)
+    block = q * q_row * jnp.exp2(dots * norm * norm_row - TAU * LOG2E) - shared
     work[...] = block + jnp.where(eye, RIDGE, 0.0)
 
-    row8 = lax.broadcasted_iota(jnp.int32, (GROUP, total), 0)
+    row8 = lax.broadcasted_iota(jnp.int32, (GROUP, LANES), 0)
+    rows8 = lax.broadcasted_iota(jnp.int32, (GROUP, total), 0)
     lane8 = lax.broadcasted_iota(jnp.int32, (GROUP, total), 1)
-
-    def step(b, carry):
+    lane_piece = lax.broadcasted_iota(jnp.int32, (PIECE, total), 1)
+
+    def spread(x):
+        return jnp.concatenate([x] * (total // LANES), axis=1)
+
+    def thirds(x):
+        parts = []
+        for _ in range(3):
+            part = x.astype(jnp.bfloat16).astype(f32)
+            parts.append(part)
+            x = x - part
+        return parts
+
+    def step(floor, b, carry):
         start = pl.multiple_of(b * GROUP, GROUP)
         rows = work[pl.ds(start, GROUP), :]
         cols = [
             jnp.broadcast_to(
                 jnp.sum(jnp.where(lane8 == start + i, rows, 0.0), axis=1, keepdims=True),
-                (GROUP, total),
+                (GROUP, LANES),
             )
             for i in range(GROUP)
         ]
-        left = jnp.where(lane8 >= start + GROUP, rows, 0.0)
-        solved = jnp.where(
+        mine = jnp.where(
             (lane8 >= start) & (lane8 < start + GROUP),
-            jnp.where(lane8 == start + row8, 1.0, 0.0),
+            jnp.where(lane8 == start + rows8, 1.0, 0.0),
             rows,
         )
-        diag = jnp.ones((GROUP, total), f32)
-        for i in range(GROUP):
-            d = cols[i][i:i + 1, :]
-            diag = jnp.where(row8 == i, d, diag)
-            m = jnp.where(row8 > i, cols[i] * (1.0 / d), 0.0)
-            for n in range(i + 1, GROUP):
-                cols[n] = cols[n] - m * cols[n][i:i + 1, :]
-            solved = solved - m * solved[i:i + 1, :]
-            left = left - m * left[i:i + 1, :]
-        scale = lax.rsqrt(diag)
-        solved = solved * scale
-        left = left * scale
+        diag = jnp.ones((GROUP, LANES), f32)
+        for i in range(0, GROUP, 2):
+            d0 = cols[i][i:i + 1, :]
+            s10 = cols[i][i + 1:i + 2, :]
+            det = d0 * cols[i + 1][i + 1:i + 2, :] - s10 * s10
+            r0 = 1.0 / d0
+            r1 = d0 * (1.0 / det)
+            diag = jnp.where(row8 == i, d0, jnp.where(row8 == i + 1, det * r0, diag))
+            for j, r in ((i, r0), (i + 1, r1)):
+                m = jnp.where(row8 > j, cols[j] * r, 0.0)
+                for n in range(j + 1, GROUP):
+                    cols[n] = cols[n] - m * cols[n][j:j + 1, :]
+                mine = mine - spread(m) * mine[j:j + 1, :]
+        mine = mine * spread(lax.rsqrt(diag))
+        left = jnp.where(lane8 >= start + GROUP, mine, 0.0)[:, floor:]
+        l0, l1, l2 = thirds(left)
+        m0, m1, m2 = thirds(mine)
         delta = lax.dot_general(
-            left, solved, (((0,), (0,)), ((), ())),
-            precision=lax.Precision.HIGHEST, preferred_element_type=f32,
-        )
-        keep = jnp.where((lane >= start) & (lane < start + GROUP), 0.0, work[...])
-        work[...] = keep - delta
-        work[pl.ds(start, GROUP), :] = solved
+            jnp.concatenate([l0, l0, l1, l1, l0, l2], axis=0).astype(jnp.bfloat16),
+            jnp.concatenate([m0, m1, m0, m1, m2, m0], axis=0).astype(jnp.bfloat16),
+            (((0,), (0,)), ((), ())), preferred_element_type=f32,
+        )
+        gone = (lane_piece >= start) & (lane_piece < start + GROUP)
+        for p in range(floor, total, PIECE):
+            work[p:p + PIECE, :] = (
+                jnp.where(gone, 0.0, work[p:p + PIECE, :]) - delta[p - floor:p - floor + PIECE, :]
+            )
+        work[pl.ds(start, GROUP), :] = mine
         return carry
 
-    lax.fori_loop(0, total // GROUP, step, 0)
-    hi, lo = split(work[...])
-    hi_ref[...] = hi
-    lo_ref[...] = lo
+    for floor in range(0, total, LANES):
+        lax.fori_loop(
+            floor // GROUP, (floor + LANES) // GROUP, functools.partial(step, floor), 0
+        )
+    hi, lo = split(jnp.where(lane <= sub, work[...], 0.0).T)
+    triple_ref[:total, :] = hi
+    triple_ref[total:2 * total, :] = lo
+    triple_ref[2 * total:, :] = hi
 
 
 def panel_kernel(
-    n_cols, rows_here, width, fac_width,
-    emb_ref, fac_ref, solved_ref, piv_ref, ids_ref, hi_ref, lo_ref, side_ref,
+    n_cols, rows_here, width,
+    emb_ref, fac_ref, solved_ref, ids_ref, turn_ref, triple_ref, side_ref,
     new_ref, gain_ref, best_ref,
+    dots_buf, shared_buf, stat_buf, sum_buf, hi_buf, lo_buf,
 ):
-    f32 = jnp.float32
+    f32, bf16 = jnp.float32, jnp.bfloat16
     total = ids_ref.shape[1]
     tile = emb_ref.shape[0]
+    fac_width = fac_ref.shape[1]
     step = pl.program_id(0)
     first = (lax.axis_index("rows") * n_cols + lax.axis_index("cols")) * rows_here + step * tile
-    piv_emb = piv_ref[:, :width]
-    piv_fac = piv_ref[:, width:width + fac_width]
-    hi_w = hi_ref[...]
-    lo_w = lo_ref[...]
     norm_row = side_ref[0:1, :]
     q_row = side_ref[1:2, :]
-    ids = ids_ref[...] - first
-    sub = lax.broadcasted_iota(jnp.int32, (LANES, LANES), 0)
-    lane = lax.broadcasted_iota(jnp.int32, (LANES, LANES), 1)
-    eye = sub == lane
-    row = lax.broadcasted_iota(jnp.int32, (SUB, total), 0)
-    q_lanes = learn(solved_ref[...])
+    here = ids_ref[...] - first
+    small_eye = lax.broadcasted_iota(jnp.int32, (LANES, LANES), 0) == lax.broadcasted_iota(
+        jnp.int32, (LANES, LANES), 1
+    )
+    ones = jnp.ones((2 * LANES, LANES), bf16)
+    eye_row = lax.broadcasted_iota(jnp.int32, (PIECE, LANES), 0)
+    eye_lane = lax.broadcasted_iota(jnp.int32, (PIECE, LANES), 1)
+    row_piece = lax.broadcasted_iota(jnp.int32, (PIECE, total), 0)
+
+    def squares(load, width, p, k):
+        acc = jnp.zeros((PIECE, LANES), f32)
+        for j in range(0, width, LANES):
+            x = load(j).astype(f32)
+            acc = acc + x * x
+        hi, lo = split(acc)
+        stat_buf[p:p + PIECE, k:k + LANES] = hi
+        stat_buf[p:p + PIECE, k + LANES:k + 2 * LANES] = lo
+
+    def row_sums(p, rows, k):
+        return jnp.dot(stat_buf[p:p + rows, k:k + 2 * LANES], ones, preferred_element_type=f32)
+
+    def line_part(x, p):
+        mine = eye_lane == eye_row + p % LANES
+        return jnp.sum(jnp.where(mine, x, 0.0), axis=0, keepdims=True)
+
+    dots_buf[...] = jnp.dot(emb_ref[...], turn_ref[:width, :], preferred_element_type=f32)
+    shared_buf[...] = jnp.dot(fac_ref[...], turn_ref[width:, :], preferred_element_type=f32)
+    for p in range(0, tile, PIECE):
+        squares(lambda j: emb_ref[p:p + PIECE, j:j + LANES], width, p, 0)
+        squares(lambda j: fac_ref[p:p + PIECE, j:j + LANES], fac_width, p, 2 * LANES)
+    sum_buf[:, :LANES] = row_sums(0, tile, 0)
+    sum_buf[:, LANES:2 * LANES] = row_sums(0, tile, 2 * LANES)
+    for g in range(tile // LANES):
+        line = solved_ref[g:g + 1, :].astype(f32)
+        counts = jnp.where(small_eye, line, 0.0).astype(bf16)
+        sum_buf[g * LANES:(g + 1) * LANES, 2 * LANES:] = jnp.dot(
+            counts, ones[:LANES, :], preferred_element_type=f32
+        )
     best = jnp.full((1, LANES), -jnp.inf, f32)
     for s in range(0, tile, SUB):
-        emb = emb_ref[s:s + SUB, :]
-        fac = fac_ref[s:s + SUB, :]
-        dots = lax.dot_general(emb, piv_emb, NT, preferred_element_type=f32)
-        shared = lax.dot_general(fac, piv_fac, NT, preferred_element_type=f32)
-        wide = emb.astype(f32)
-        norm = lax.rsqrt(jnp.sum(wide * wide, axis=1, keepdims=True) / width + EPS)
-        widef = fac.astype(f32)
-        used = jnp.sum(widef * widef, axis=1, keepdims=True)
-        q = jnp.concatenate(
-            [
-                jnp.sum(
-                    jnp.where(eye, q_lanes[g:g + 1, :], 0.0), axis=1, keepdims=True
+        for p in range(s, s + SUB, PIECE):
+            rows = slice(p, p + PIECE)
+            norm = lax.rsqrt(sum_buf[rows, :LANES] / width + EPS)
+            q = learn(sum_buf[rows, 2 * LANES:])
+            for k in range(0, total, LANES):
+                half = slice(k, k + LANES)
+                power = dots_buf[rows, half] * norm * norm_row[:, half] - TAU * LOG2E
+                panel = q * q_row[:, half] * jnp.exp2(power) - shared_buf[rows, half]
+                panel = jnp.where(row_piece[:, half] == here[:, half] - p, panel + RIDGE, panel)
+                hi, lo = split(panel)
+                hi_buf[rows, half] = hi
+                lo_buf[rows, half] = lo
+        sub = slice(s, s + SUB)
+        dots_buf[sub, :] = jnp.dot(
+            jnp.concatenate([hi_buf[sub, :], hi_buf[sub, :], lo_buf[sub, :]], axis=1),
+            triple_ref[...], preferred_element_type=f32,
+        )
+        for p in range(s, s + SUB, PIECE):
+            new_ref[p:p + PIECE, :] = dots_buf[p:p + PIECE, :].astype(bf16)
+            squares(lambda j: dots_buf[p:p + PIECE, j:j + LANES], total, p, 0)
+        sum_buf[sub, :LANES] = row_sums(s, SUB, 0)
+        for g in range(s // LANES, (s + SUB) // LANES):
+            line = jnp.zeros((1, LANES), f32)
+            for p in range(g * LANES, (g + 1) * LANES, PIECE):
+                rows = slice(p, p + PIECE)
+                q = learn(sum_buf[rows, 2 * LANES:])
+                line = line + line_part(
+                    q * q + RIDGE - sum_buf[rows, LANES:2 * LANES] - sum_buf[rows, :LANES], p
                 )
-                for g in range(s // LANES, (s + SUB) // LANES)
-            ],
-            axis=0,
-        )
-        panel = q * q_row * jnp.exp(dots * norm * norm_row - TAU) - shared
-        panel = jnp.where(row + s == ids, panel + RIDGE, panel)
-        hi, lo = split(panel)
-        full = (
-            lax.dot_general(hi, hi_w, NT, preferred_element_type=f32)
-            + lax.dot_general(hi, lo_w, NT, preferred_element_type=f32)
-            + lax.dot_general(lo, hi_w, NT, preferred_element_type=f32)
-        )
-        new_ref[s:s + SUB, :] = full.astype(jnp.bfloat16)
-        gain = q * q + RIDGE - used - jnp.sum(full * full, axis=1, keepdims=True)
-        for g in range(0, SUB, LANES):
-            line = jnp.sum(jnp.where(eye, gain[g:g + LANES, :], 0.0), axis=0, keepdims=True)
-            at = (s + g) // LANES
-            gain_ref[at:at + 1, :] = line
+            gain_ref[g:g + 1, :] = line
             best = jnp.maximum(best, line)
     best = jnp.broadcast_to(best, best_ref.shape)
 
@@ -377,17 +437,19 @@
         name="gather",
     )(own)
     ids = pivots.reshape(1, total)
-    piv, hi, lo, side = pl.pallas_call(
+    turn, triple, side = pl.pallas_call(
         functools.partial(factor_kernel, rows_here, width, fac_width),
         out_shape=[
-            jax.ShapeDtypeStruct((total, packet), bf16),
-            jax.ShapeDtypeStruct((total, total), bf16),
-            jax.ShapeDtypeStruct((total, total), bf16),
+            jax.ShapeDtypeStruct((width + fac_width, total), bf16),
+            jax.ShapeDtypeStruct((3 * total, total), bf16),
             jax.ShapeDtypeStruct((8, total), jnp.float32),
         ],
         in_specs=[vmem, vmem],
-        out_specs=[vmem] * 4,
-        scratch_shapes=[pltpu.VMEM((total, total), jnp.float32)],
+        out_specs=[vmem] * 3,
+        scratch_shapes=[
+            pltpu.VMEM((total, packet), bf16),
+            pltpu.VMEM((total, total), jnp.float32),
+        ],
         compiler_params=params(),
         name="factor",
     )(ids, everyone.reshape(devices * PMAX, packet))
@@ -398,7 +460,7 @@
         return pl.BlockSpec(shape, lambda t: (0, 0))
 
     new_cols, gains, best = pl.pallas_call(
-        functools.partial(panel_kernel, n_cols, rows_here, width, fac_width),
+        functools.partial(panel_kernel, n_cols, rows_here, width),
         out_shape=[
             jax.ShapeDtypeStruct((rows_here, total), bf16),
             jax.ShapeDtypeStruct((lines, LANES), jnp.float32),
@@ -409,10 +471,9 @@
             pl.BlockSpec((tile, width), lambda t: (t, 0)),
             pl.BlockSpec((tile, fac_width), lambda t: (t, 0)),
             pl.BlockSpec((tile // LANES, LANES), lambda t: (t, 0)),
-            whole((total, packet)),
             whole((1, total)),
-            whole((total, total)),
-            whole((total, total)),
+            whole((width + fac_width, total)),
+            whole((3 * total, total)),
             whole((8, total)),
         ],
         out_specs=[
@@ -420,9 +481,17 @@
             pl.BlockSpec((tile // LANES, LANES), lambda t: (t, 0)),
             whole((8, LANES)),
         ],
+        scratch_shapes=[
+            pltpu.VMEM((tile, total), jnp.float32),
+            pltpu.VMEM((tile, total), jnp.float32),
+            pltpu.VMEM((tile, 4 * LANES), bf16),
+            pltpu.VMEM((tile, 3 * LANES), jnp.float32),
+            pltpu.VMEM((tile, total), bf16),
+            pltpu.VMEM((tile, total), bf16),
+        ],
         compiler_params=params(),
         name="panel",
-    )(embeddings, factor_cols, solved.reshape(lines, LANES), piv, ids, hi, lo, side)
+    )(embeddings, factor_cols, solved.reshape(lines, LANES), ids, turn, triple, side)
     top = pl.pallas_call(
         functools.partial(best_kernel, n_rows, n_cols),
         out_shape=jax.ShapeDtypeStruct((1, 1), jnp.float32),

time: 82.3 us -> 81.5 us (level)
    pallas_call x1, Pallas kernels: 21.9 us -> 14.9 us  [body(): pl.pallas_call(functools.partial(factor_kernel, rows_here, width, fac_wid...]
    pallas_call x1, Pallas kernels: 21.4 us -> 27.6 us  [body(): pl.pallas_call(functools.partial(panel_kernel, n_cols, rows_here, width),...]
where the time goes in v5:
time: 81.5 us; the launch traced here: 81.4 us
  Pallas kernels  79 us (97%)
  between operations  2.41 us (3%)
    pallas_call x1, Pallas kernels, body(): pl.pallas_call(functools.partial(panel_kernel, n_cols, rows_here, width),...  27.6 us
    pallas_call x1, Pallas kernels, body(): pl.pallas_call(functools.partial(gather_kernel, n_rows, n_cols), out_shap...  22.1 us
    pallas_call x1, Pallas kernels, body(): pl.pallas_call(functools.partial(factor_kernel, rows_here, width, fac_wid...  14.9 us
    pallas_call x1, Pallas kernels, body(): pl.pallas_call(functools.partial(best_kernel, n_rows, n_cols), out_shape=...  10.7 us
    pallas_call x1, Pallas kernels, body(): pl.pallas_call(functools.partial(pick_kernel, n_cols), out_shape=jax.Shap...  3.71 us

profile of v5, /device:TPU:0, one launch (start us, length us, event | category | flops | bytes accessed | tf_op | source)
XLA Modules:
  0.0 81.4 jit_solution(14374139714260762711)
XLA Ops:
  0.6 3.7 %pick.1.own_ref = bf16[16,1664]{1,0:T(8,128)(2,1)} custom-call(s32[256]{0:T(256)} %piv_ref.1, s32[7168]{0:T(1024)} %solved_ref.1, bf16[7168,1024]{1,0:T(8,128)(2,1)} %emb_ref.3, bf16[7168,512]{1,0:T(8,128)(2,1)} %fac_ref.3), custom_call_target="tpu_custom_call" | custom-call | tf_op jit(solution)/shard_map/pick/pallas_call | solution.py:413
  4.3 22.1 %gather.1 = bf16[32,16,1664]{2,1,0:T(8,128)(2,1)} custom-call(bf16[16,1664]{1,0:T(8,128)(2,1)} %pick.1.own_ref), custom_call_target="tpu_custom_call" | custom-call | tf_op jit(solution)/shard_map/gather/pallas_call | solution.py:426
  26.4 14.9 %factor.1 = (bf16[1536,256]{1,0:T(8,128)(2,1)}, bf16[768,256]{1,0:T(8,128)(2,1)}, f32[8,256]{1,0:T(8,128)}) custom-call(s32[1,256]{1,0:T(1,128)} %bitcast.7, bf16[512,1664]{1,0:T(8,128)(2,1)} %bitcast.5), custom_call_target="tpu_custom_call" | custom-call | tf_op jit(solution)/shard_map/factor/pallas_call | solution.py:440
  41.3 27.6 %panel.1 = (bf16[7168,256]{1,0:T(8,128)(2,1)}, f32[56,128]{1,0:T(8,128)}, f32[8,128]{1,0:T(8,128)}) custom-call(bf16[7168,1024]{1,0:T(8,128)(2,1)} %emb_ref.3, bf16[7168,512]{1,0:T(8,128)(2,1)} %fac_ref.3, s32[56,128]{1,0:T(8,128)} %bitcast.6, s32[1,256]{1,0:T(1,128)} %bitcast.8, bf16[1536,256]{1,0:T(8,128)(2,1)} %get-tuple-element.9.turn_ref, ...), custom_call_target="tpu_custom_call" | custom-call | tf_op jit(solution)/shard_map/panel/pallas_call | solution.py:462
  68.9 10.7 %best.1 = f32[1,1]{1,0:T(1,128)} custom-call(f32[8,128]{1,0:T(8,128)} %get-tuple-element.14.own_ref), custom_call_target="tpu_custom_call" | custom-call | tf_op jit(solution)/shard_map/best/pallas_call | solution.py:495

commit v6 on v5

--- a/solution.py
+++ b/solution.py
@@ -19,7 +19,6 @@
 PIECE = 32
 VMEM_LIMIT = 56 * 1024 * 1024
 MESH = pl.DeviceIdType.MESH
-NT = (((1,), (1,)), ((), ()))
 
 
 def learn(counts):
@@ -274,89 +273,53 @@
 
 
 def panel_kernel(
-    n_cols, rows_here, width,
-    emb_ref, fac_ref, solved_ref, ids_ref, turn_ref, triple_ref, side_ref,
+    n_cols, rows_here, width, emb_ref, fac_ref, solved_ref, ids_ref, turn_ref, triple_ref, side_ref,
     new_ref, gain_ref, best_ref,
-    dots_buf, shared_buf, stat_buf, sum_buf, hi_buf, lo_buf,
 ):
-    f32, bf16 = jnp.float32, jnp.bfloat16
+    f32 = jnp.float32
     total = ids_ref.shape[1]
     tile = emb_ref.shape[0]
-    fac_width = fac_ref.shape[1]
     step = pl.program_id(0)
     first = (lax.axis_index("rows") * n_cols + lax.axis_index("cols")) * rows_here + step * tile
     norm_row = side_ref[0:1, :]
     q_row = side_ref[1:2, :]
-    here = ids_ref[...] - first
-    small_eye = lax.broadcasted_iota(jnp.int32, (LANES, LANES), 0) == lax.broadcasted_iota(
-        jnp.int32, (LANES, LANES), 1
-    )
-    ones = jnp.ones((2 * LANES, LANES), bf16)
-    eye_row = lax.broadcasted_iota(jnp.int32, (PIECE, LANES), 0)
-    eye_lane = lax.broadcasted_iota(jnp.int32, (PIECE, LANES), 1)
-    row_piece = lax.broadcasted_iota(jnp.int32, (PIECE, total), 0)
-
-    def squares(load, width, p, k):
-        acc = jnp.zeros((PIECE, LANES), f32)
-        for j in range(0, width, LANES):
-            x = load(j).astype(f32)
-            acc = acc + x * x
-        hi, lo = split(acc)
-        stat_buf[p:p + PIECE, k:k + LANES] = hi
-        stat_buf[p:p + PIECE, k + LANES:k + 2 * LANES] = lo
-
-    def row_sums(p, rows, k):
-        return jnp.dot(stat_buf[p:p + rows, k:k + 2 * LANES], ones, preferred_element_type=f32)
-
-    def line_part(x, p):
-        mine = eye_lane == eye_row + p % LANES
-        return jnp.sum(jnp.where(mine, x, 0.0), axis=0, keepdims=True)
-
-    dots_buf[...] = jnp.dot(emb_ref[...], turn_ref[:width, :], preferred_element_type=f32)
-    shared_buf[...] = jnp.dot(fac_ref[...], turn_ref[width:, :], preferred_element_type=f32)
-    for p in range(0, tile, PIECE):
-        squares(lambda j: emb_ref[p:p + PIECE, j:j + LANES], width, p, 0)
-        squares(lambda j: fac_ref[p:p + PIECE, j:j + LANES], fac_width, p, 2 * LANES)
-    sum_buf[:, :LANES] = row_sums(0, tile, 0)
-    sum_buf[:, LANES:2 * LANES] = row_sums(0, tile, 2 * LANES)
-    for g in range(tile // LANES):
-        line = solved_ref[g:g + 1, :].astype(f32)
-        counts = jnp.where(small_eye, line, 0.0).astype(bf16)
-        sum_buf[g * LANES:(g + 1) * LANES, 2 * LANES:] = jnp.dot(
-            counts, ones[:LANES, :], preferred_element_type=f32
-        )
+    ids = ids_ref[...] - first
+    sub = lax.broadcasted_iota(jnp.int32, (LANES, LANES), 0)
+    lane = lax.broadcasted_iota(jnp.int32, (LANES, LANES), 1)
+    eye = sub == lane
+    row = lax.broadcasted_iota(jnp.int32, (SUB, total), 0)
+    q_lanes = learn(solved_ref[...])
     best = jnp.full((1, LANES), -jnp.inf, f32)
     for s in range(0, tile, SUB):
-        for p in range(s, s + SUB, PIECE):
-            rows = slice(p, p + PIECE)
-            norm = lax.rsqrt(sum_buf[rows, :LANES] / width + EPS)
-            q = learn(sum_buf[rows, 2 * LANES:])
-            for k in range(0, total, LANES):
-                half = slice(k, k + LANES)
-                power = dots_buf[rows, half] * norm * norm_row[:, half] - TAU * LOG2E
-                panel = q * q_row[:, half] * jnp.exp2(power) - shared_buf[rows, half]
-                panel = jnp.where(row_piece[:, half] == here[:, half] - p, panel + RIDGE, panel)
-                hi, lo = split(panel)
-                hi_buf[rows, half] = hi
-                lo_buf[rows, half] = lo
-        sub = slice(s, s + SUB)
-        dots_buf[sub, :] = jnp.dot(
-            jnp.concatenate([hi_buf[sub, :], hi_buf[sub, :], lo_buf[sub, :]], axis=1),
-            triple_ref[...], preferred_element_type=f32,
-        )
-        for p in range(s, s + SUB, PIECE):
-            new_ref[p:p + PIECE, :] = dots_buf[p:p + PIECE, :].astype(bf16)
-            squares(lambda j: dots_buf[p:p + PIECE, j:j + LANES], total, p, 0)
-        sum_buf[sub, :LANES] = row_sums(s, SUB, 0)
-        for g in range(s // LANES, (s + SUB) // LANES):
-            line = jnp.zeros((1, LANES), f32)
-            for p in range(g * LANES, (g + 1) * LANES, PIECE):
-                rows = slice(p, p + PIECE)
-                q = learn(sum_buf[rows, 2 * LANES:])
-                line = line + line_part(
-                    q * q + RIDGE - sum_buf[rows, LANES:2 * LANES] - sum_buf[rows, :LANES], p
+        emb = emb_ref[s:s + SUB, :]
+        fac = fac_ref[s:s + SUB, :]
+        dots = jnp.dot(emb, turn_ref[:width, :], preferred_element_type=f32)
+        shared = jnp.dot(fac, turn_ref[width:, :], preferred_element_type=f32)
+        wide = emb.astype(f32)
+        norm = lax.rsqrt(jnp.sum(wide * wide, axis=1, keepdims=True) / width + EPS)
+        widef = fac.astype(f32)
+        used = jnp.sum(widef * widef, axis=1, keepdims=True)
+        q = jnp.concatenate(
+            [
+                jnp.sum(
+                    jnp.where(eye, q_lanes[g:g + 1, :], 0.0), axis=1, keepdims=True
                 )
-            gain_ref[g:g + 1, :] = line
+                for g in range(s // LANES, (s + SUB) // LANES)
+            ],
+            axis=0,
+        )
+        panel = q * q_row * jnp.exp2(dots * norm * norm_row - TAU * LOG2E) - shared
+        panel = jnp.where(row + s == ids, panel + RIDGE, panel)
+        hi, lo = split(panel)
+        full = jnp.dot(
+            jnp.concatenate([hi, hi, lo], axis=1), triple_ref[...], preferred_element_type=f32
+        )
+        new_ref[s:s + SUB, :] = full.astype(jnp.bfloat16)
+        gain = q * q + RIDGE - used - jnp.sum(full * full, axis=1, keepdims=True)
+        for g in range(0, SUB, LANES):
+            line = jnp.sum(jnp.where(eye, gain[g:g + LANES, :], 0.0), axis=0, keepdims=True)
+            at = (s + g) // LANES
+            gain_ref[at:at + 1, :] = line
             best = jnp.maximum(best, line)
     best = jnp.broadcast_to(best, best_ref.shape)
 
@@ -481,14 +444,6 @@
             pl.BlockSpec((tile // LANES, LANES), lambda t: (t, 0)),
             whole((8, LANES)),
         ],
-        scratch_shapes=[
-            pltpu.VMEM((tile, total), jnp.float32),
-            pltpu.VMEM((tile, total), jnp.float32),
-            pltpu.VMEM((tile, 4 * LANES), bf16),
-            pltpu.VMEM((tile, 3 * LANES), jnp.float32),
-            pltpu.VMEM((tile, total), bf16),
-            pltpu.VMEM((tile, total), bf16),
-        ],
         compiler_params=params(),
         name="panel",
     )(embeddings, factor_cols, solved.reshape(lines, LANES), ids, turn, triple, side)

time: 81.5 us -> 75.9 us (0.931)
  Pallas kernels: 79 us -> 73.1 us
    pallas_call x1, Pallas kernels: 27.6 us -> 22 us  [body(): pl.pallas_call(functools.partial(panel_kernel, n_cols, rows_here, width),...]
where the time goes in v6:
time: 75.9 us; the launch traced here: 75.5 us
  Pallas kernels  73.1 us (96%)
  between operations  2.41 us (3%)
    pallas_call x1, Pallas kernels, body(): pl.pallas_call(functools.partial(gather_kernel, n_rows, n_cols), out_shap...  22.3 us
    pallas_call x1, Pallas kernels, body(): pl.pallas_call(functools.partial(panel_kernel, n_cols, rows_here, width),...  22 us
    pallas_call x1, Pallas kernels, body(): pl.pallas_call(functools.partial(factor_kernel, rows_here, width, fac_wid...  14.9 us
    pallas_call x1, Pallas kernels, body(): pl.pallas_call(functools.partial(best_kernel, n_rows, n_cols), out_shape=...  10.2 us
    pallas_call x1, Pallas kernels, body(): pl.pallas_call(functools.partial(pick_kernel, n_cols), out_shape=jax.Shap...  3.67 us

profile of v6, /device:TPU:0, one launch (start us, length us, event | category | flops | bytes accessed | tf_op | source)
XLA Modules:
  0.0 75.5 jit_solution(8803913238986137590)
XLA Ops:
  0.6 3.7 %pick.1.own_ref = bf16[16,1664]{1,0:T(8,128)(2,1)} custom-call(s32[256]{0:T(256)} %piv_ref.1, s32[7168]{0:T(1024)} %solved_ref.1, bf16[7168,1024]{1,0:T(8,128)(2,1)} %emb_ref.3, bf16[7168,512]{1,0:T(8,128)(2,1)} %fac_ref.3), custom_call_target="tpu_custom_call" | custom-call | tf_op jit(solution)/shard_map/pick/pallas_call | solution.py:376
  4.3 22.3 %gather.1 = bf16[32,16,1664]{2,1,0:T(8,128)(2,1)} custom-call(bf16[16,1664]{1,0:T(8,128)(2,1)} %pick.1.own_ref), custom_call_target="tpu_custom_call" | custom-call | tf_op jit(solution)/shard_map/gather/pallas_call | solution.py:389
  26.6 14.9 %factor.1 = (bf16[1536,256]{1,0:T(8,128)(2,1)}, bf16[768,256]{1,0:T(8,128)(2,1)}, f32[8,256]{1,0:T(8,128)}) custom-call(s32[1,256]{1,0:T(1,128)} %bitcast.7, bf16[512,1664]{1,0:T(8,128)(2,1)} %bitcast.5), custom_call_target="tpu_custom_call" | custom-call | tf_op jit(solution)/shard_map/factor/pallas_call | solution.py:403
  41.5 22.0 %panel.1 = (bf16[7168,256]{1,0:T(8,128)(2,1)}, f32[56,128]{1,0:T(8,128)}, f32[8,128]{1,0:T(8,128)}) custom-call(bf16[7168,1024]{1,0:T(8,128)(2,1)} %emb_ref.3, bf16[7168,512]{1,0:T(8,128)(2,1)} %fac_ref.3, s32[56,128]{1,0:T(8,128)} %bitcast.6, s32[1,256]{1,0:T(1,128)} %bitcast.8, bf16[1536,256]{1,0:T(8,128)(2,1)} %get-tuple-element.9.turn_ref, ...), custom_call_target="tpu_custom_call" | custom-call | tf_op jit(solution)/shard_map/panel/pallas_call | solution.py:425
  63.5 10.2 %best.1 = f32[1,1]{1,0:T(1,128)} custom-call(f32[8,128]{1,0:T(8,128)} %get-tuple-element.14.own_ref), custom_call_target="tpu_custom_call" | custom-call | tf_op jit(solution)/shard_map/best/pallas_call | solution.py:450
